TPU v7x, 512 devices: a whole 4x4x16 slice. The times are simulated.
512 devices in a mesh: gx: 32 (over y, z_hi, core), gy: 16 (over x, z_lo).
Axes of the slice: x: 4, y: 4, z: 16 (z_hi: 4, z_lo: 4; z = z_hi * 4 + z_lo), core: 2. Of those that a mesh axis runs over, the one named last changes fastest.
Arguments:
- pressure: float32 [512, 98304], P('gx', 'gy'), may hold values from -6 to 6
- previous: float32 [512, 98304], P('gx', 'gy'), may hold values from -6 to 6
- velocity: bfloat16 [512, 98304], P('gx', 'gy'), may hold values from 0.039794922 to 0.19921875
- tucker_core: bfloat16 [3, 384, 12288], P(None, 'gx', 'gy'), may hold values from -6 to 6
- first_factor: bfloat16 [512, 384], P('gx'), may hold values from -0.3125 to 0.3125
- second_factor: bfloat16 [1536, 384], P('gy'), may hold values from -0.3125 to 0.3125
- depth_factor: bfloat16 [64, 32], replicated, may hold values from -1 to 1
Outputs:
- image: float32 [512, 98304], P('gx', 'gy')
All inputs are finite; a program needn't handle non-finite values.
Results may differ from a plain program's by a relative error of at most 0.00035.
Values may be sent and summed in bfloat16 or wider, within the bound.
A program may use at most 192 MiB of HBM per device.

v0:
```python
import jax
import jax.numpy as jnp
from jax import lax
from jax.sharding import PartitionSpec as P

STENCIL = (-205.0 / 72.0, 8.0 / 5.0, -1.0 / 5.0, 8.0 / 315.0, -1.0 / 560.0)
HIGH = lax.Precision.HIGHEST


def with_halo(cells, sides, width):
    for axis, dim in sides:
        count = lax.axis_size(axis)
        ends = count - 1
        head = lax.slice_in_dim(cells, 0, width, axis=dim)
        tail = lax.slice_in_dim(cells, cells.shape[dim] - width, cells.shape[dim], axis=dim)
        cells = jnp.concatenate(
            [
                lax.ppermute(tail, axis, [(i, (i + 1) % count) for i in range(ends)]),
                cells,
                lax.ppermute(head, axis, [((i + 1) % count, i) for i in range(ends)]),
            ],
            axis=dim,
        )
    return cells


def laplace(field, depth_cells):
    lines, flat = field.shape
    margin = 4 * depth_cells
    wide_rows = with_halo(field, (("gx", 0),), 4)
    wide_cols = with_halo(field, (("gy", 1),), margin)
    level = lax.broadcasted_iota(jnp.int32, (1, flat), 1) % depth_cells
    blank = jnp.zeros_like(field)
    total = 3.0 * STENCIL[0] * field
    for reach in range(1, 5):
        near = wide_rows[4 + reach : 4 + reach + lines] + wide_rows[4 - reach : 4 - reach + lines]
        lift = reach * depth_cells
        near = (
            near
            + wide_cols[:, margin + lift : margin + lift + flat]
            + wide_cols[:, margin - lift : margin - lift + flat]
        )
        deeper = jnp.concatenate([field[:, reach:], blank[:, :reach]], axis=1)
        higher = jnp.concatenate([blank[:, :reach], field[:, : flat - reach]], axis=1)
        near = (
            near
            + jnp.where(level + reach < depth_cells, deeper, 0.0)
            + jnp.where(level >= reach, higher, 0.0)
        )
        total = total + STENCIL[reach] * near
    return total


def expand(blocks, first_factor, second_factor, depth_factor):
    count, rows_first, rows_second, rank_depth = blocks.shape
    cells_x = first_factor.shape[0]
    cells_y = second_factor.shape[0]
    columns = first_factor
    partial_value = jnp.einsum(
        "xr,srnc->sxnc",
        columns,
        lax.all_gather(blocks, "gx", axis=1, tiled=True),
        preferred_element_type=jnp.float32,
    )
    columns = second_factor.astype(jnp.float32)
    mixed = jnp.einsum(
        "yn,sxnc->sxyc",
        columns,
        lax.all_gather(partial_value, "gy", axis=2, tiled=True),
        precision=HIGH,
    )
    field = jnp.einsum("sxyc,zc->sxyz", mixed, depth_factor.astype(jnp.float32), precision=HIGH)
    return field.reshape(count, cells_x, cells_y * depth_factor.shape[0])


def body(pressure, previous, velocity, tucker_core, first_factor, second_factor, depth_factor):
    depth_cells = depth_factor.shape[0]
    rank_depth = depth_factor.shape[1]
    steps_all = tucker_core.shape[0]
    local_second = tucker_core.shape[2] // rank_depth
    core_blocks = tucker_core.reshape(steps_all, tucker_core.shape[1], local_second, rank_depth)
    speed = velocity.astype(jnp.float32)
    group = 1
    current = pressure
    before = previous
    image = jnp.zeros(pressure.shape, jnp.float32)
    sources = None
    for section in range(steps_all):
        sources = expand(
            core_blocks[section : section + group], first_factor, second_factor, depth_factor
        )
        following = 2.0 * current - before + speed * laplace(current, depth_cells)
        image = image + sources[section % group] * following
        before = current
        current = following
    return image


def solution(mesh):
    placed = (
        P("gx", "gy"),
        P("gx", "gy"),
        P("gx", "gy"),
        P(None, "gx", "gy"),
        P("gx", None),
        P("gy", None),
        P(),
    )
    return jax.shard_map(body, mesh=mesh, in_specs=placed, out_specs=P("gx", "gy"), check_vma=False)
```

profile of v0, /device:TPU:1, one launch (start us, length us, event | category | flops | bytes accessed | tf_op | source)
XLA Modules:
  0.0 604.6 jit_solution(1643792092244026916)
XLA Ops:
  2.7 5.6 collective-permute-start.3
  10.0 8.3 %collective-permute-start = (f32[4,6144]{1,0:T(4,128)}, f32[4,6144]{1,0:T(4,128)}, u32[]{:S(2)}, u32[]{:S(2)}) collective-permute-start(f32[4,6144]{1,0:T(4,128)} %get-tuple-element.37), channel_id=1, source_target_pairs={{16,0},{32,16},{48,32},{64,48},{80,64},{96,80},{112,96},{128,112},... | collective-permute-start | bytes 294920 | tf_op jit(solution)/shard_map/ppermute | solution.py:20
  18.4 3.3 collective-permute-start.1
  21.8 2.1 fusion.151
  23.9 2.1 fusion.154
  29.0 91.4 %all_gather.20 = bf16[1,384,24,32]{3,2,0,1:T(8,128)(2,1)S(1)} all-gather(bf16[1,12,24,32]{3,2,0,1:T(8,128)(2,1)S(1)} %slice.349), channel_id=1, replica_groups=mesh['gx'=32,'gy'=16] {'gx'}, dimensions={1}, use_global_device_ids=true | all-gather | bytes 608256 | tf_op jit(solution)/shard_map/all_gather | solution.py:62
  122.1 74.5 %all_gather.22 = bf16[1,384,24,32]{3,2,0,1:T(8,128)(2,1)S(1)} all-gather(bf16[1,12,24,32]{3,2,0,1:T(8,128)(2,1)} %slice.379), channel_id=1, replica_groups=mesh['gx'=32,'gy'=16] {'gx'}, dimensions={1}, use_global_device_ids=true | all-gather | bytes 608256 | tf_op jit(solution)/shard_map/all_gather | solution.py:62
  196.7 2.4 copy.31
  200.4 2.4 convolution_bitcast_fusion.3
  202.8 94.0 %all_gather.18 = bf16[1,384,24,32]{3,2,0,1:T(8,128)(2,1)S(1)} all-gather(bf16[1,12,24,32]{3,2,0,1:T(8,128)(2,1)S(1)} %slice.319), channel_id=1, replica_groups=mesh['gx'=32,'gy'=16] {'gx'}, dimensions={1}, use_global_device_ids=true | all-gather | bytes 608256 | tf_op jit(solution)/shard_map/all_gather | solution.py:62
  299.0 78.5 %all_gather.19 = f32[1,16,384,32]{3,1,0,2:T(8,128)} all-gather(f32[1,16,24,32]{3,1,0,2:T(8,128)S(1)} %convolution_bitcast_fusion.5), channel_id=1, replica_groups=mesh['gx'=32,'gy'=16] {'gy'}, dimensions={2}, use_global_device_ids=true | all-gather | bytes 835584 | tf_op jit(solution)/shard_map/all_gather | solution.py:69
  377.6 2.3 copy.25
  379.9 75.6 %all_gather.23 = f32[1,16,384,32]{3,1,0,2:T(8,128)} all-gather(f32[1,16,24,32]{3,1,0,2:T(8,128)S(1)} %copy-done.12), channel_id=1, replica_groups=mesh['gx'=32,'gy'=16] {'gy'}, dimensions={2}, use_global_device_ids=true | all-gather | bytes 835584 | tf_op jit(solution)/shard_map/all_gather | solution.py:69
  455.6 2.3 copy.33
  460.6 74.6 %all_gather.21 = f32[1,16,384,32]{3,1,0,2:T(8,128)} all-gather(f32[1,16,24,32]{3,1,0,2:T(8,128)S(1)} %copy-done.11), channel_id=1, replica_groups=mesh['gx'=32,'gy'=16] {'gy'}, dimensions={2}, use_global_device_ids=true | all-gather | bytes 835584 | tf_op jit(solution)/shard_map/all_gather | solution.py:69
  535.2 2.3 copy.29
  544.5 2.8 fusion.6
  549.3 4.0 collective-permute-start.7
  553.2 20.9 %collective-permute-start.4 = (f32[4,6144]{1,0:T(4,128)S(1)}, f32[4,6144]{1,0:T(4,128)S(1)}, u32[]{:S(2)}, u32[]{:S(2)}) collective-permute-start(f32[4,6144]{1,0:T(4,128)S(1)} %get-tuple-element.25), channel_id=1, source_target_pairs={{16,0},{32,16},{48,32},{64,48},{80,64},{96,80},{112,96},{128,112},... | collective-permute-start | bytes 294920 | tf_op jit(solution)/shard_map/ppermute | solution.py:20
  574.1 3.0 collective-permute-start.5
  580.4 1.9 fusion.7
  584.3 4.0 collective-permute-start.11
  590.2 8.9 %collective-permute-start.9 = (f32[4,6144]{1,0:T(4,128)S(1)}, f32[4,6144]{1,0:T(4,128)S(1)}, u32[]{:S(2)}, u32[]{:S(2)}) collective-permute-start(f32[4,6144]{1,0:T(4,128)S(1)} %get-tuple-element.14), channel_id=1, source_target_pairs={{0,16},{16,32},{32,48},{48,64},{64,80},{80,96},{96,112},{112,128},... | collective-permute-start | bytes 294920 | tf_op jit(solution)/shard_map/ppermute | solution.py:18
  601.9 2.7 fusion.10
  (89 shorter events, 34.0 us)
Async XLA Ops:
  0.0 457.9 %copy-start = (bf16[96,384]{1,0:T(8,128)(2,1)S(1)}, bf16[96,384]{1,0:T(8,128)(2,1)}, u32[]{:S(2)}) copy-start(bf16[96,384]{1,0:T(8,128)(2,1)} %param.12) | copy-start | bytes 221188
  0.0 26.0 %copy-start.1 = (f32[16,6144]{1,0:T(8,128)S(1)}, f32[16,6144]{1,0:T(8,128)}, u32[]{:S(2)}) copy-start(f32[16,6144]{1,0:T(8,128)} %param.7) | copy-start | bytes 1179652
  1.4 541.4 %collective-permute-start.2 = (f32[16,256]{1,0:T(8,128)}, f32[16,256]{1,0:T(8,128)}, u32[]{:S(2)}, u32[]{:S(2)}) collective-permute-start(f32[16,256]{1,0:T(8,128)} %get-tuple-element.42), channel_id=1, source_target_pairs={{1,0},{2,1},{3,2},{4,3},{5,4},{6,5},{7,6},{8,7},{9,8},{10,9},{11,1... | collective-permute-start | bytes 49160 | tf_op jit(solution)/shard_map/ppermute | solution.py:20
  2.7 539.3 %collective-permute-start.3 = (f32[16,256]{1,0:T(8,128)}, f32[16,256]{1,0:T(8,128)}, u32[]{:S(2)}, u32[]{:S(2)}) collective-permute-start(f32[16,256]{1,0:T(8,128)} %get-tuple-element.43), channel_id=1, source_target_pairs={{0,1},{1,2},{2,3},{3,4},{4,5},{5,6},{6,7},{7,8},{8,9},{9,10},{10,1... | collective-permute-start | bytes 49160 | tf_op jit(solution)/shard_map/ppermute | solution.py:18
  10.0 533.5 %collective-permute-start = (f32[4,6144]{1,0:T(4,128)}, f32[4,6144]{1,0:T(4,128)}, u32[]{:S(2)}, u32[]{:S(2)}) collective-permute-start(f32[4,6144]{1,0:T(4,128)} %get-tuple-element.37), channel_id=1, source_target_pairs={{16,0},{32,16},{48,32},{64,48},{80,64},{96,80},{112,96},{128,112},... | collective-permute-start | bytes 294920 | tf_op jit(solution)/shard_map/ppermute | solution.py:20
  18.4 526.1 %collective-permute-start.1 = (f32[4,6144]{1,0:T(4,128)}, f32[4,6144]{1,0:T(4,128)}, u32[]{:S(2)}, u32[]{:S(2)}) collective-permute-start(f32[4,6144]{1,0:T(4,128)} %get-tuple-element.38), channel_id=1, source_target_pairs={{0,16},{16,32},{32,48},{48,64},{64,80},{80,96},{96,112},{112,128},... | collective-permute-start | bytes 294920 | tf_op jit(solution)/shard_map/ppermute | solution.py:18
  21.8 6.3 %copy-start.15 = (bf16[3,12,768]{2,1,0:T(8,128)(2,1)S(1)}, bf16[3,12,768]{2,1,0:T(8,128)(2,1)}, u32[]{:S(2)}) copy-start(bf16[3,12,768]{2,1,0:T(8,128)(2,1)} %param.10) | copy-start | bytes 165892
  122.1 77.0 %copy-start.13 = (bf16[16,384]{1,0:T(8,128)(2,1)S(1)}, bf16[16,384]{1,0:T(8,128)(2,1)}, u32[]{:S(2)}) copy-start(bf16[16,384]{1,0:T(8,128)(2,1)} %param.11) | copy-start | bytes 36868
  299.0 80.9 %copy-start.12 = (f32[1,16,24,32]{3,1,0,2:T(8,128)S(1)}, f32[1,16,24,32]{3,1,0,2:T(8,128)}, u32[]{:S(2)}) copy-start(f32[1,16,24,32]{3,1,0,2:T(8,128)} %convolution_bitcast_fusion.3) | copy-start | bytes 147460
  538.0 6.5 %copy-start.2 = (bf16[16,6144]{1,0:T(8,128)(2,1)S(1)}, bf16[16,6144]{1,0:T(8,128)(2,1)}, u32[]{:S(2)}) copy-start(bf16[16,6144]{1,0:T(8,128)(2,1)} %param.9) | copy-start | bytes 589828
  538.0 6.5 %copy-start.3 = (f32[16,6143]{1,0:T(8,128)S(1)}, f32[16,6143]{1,0:T(8,128)}, u32[]{:S(2)}) copy-start(f32[16,6143]{1,0:T(8,128)} %get-tuple-element.29) | copy-start | bytes 1179460
  539.9 4.6 copy-start.4
  539.9 4.6 copy-start.5
  548.0 29.4 %collective-permute-start.6 = (f32[16,256]{1,0:T(8,128)S(1)}, f32[16,256]{1,0:T(8,128)S(1)}, u32[]{:S(2)}, u32[]{:S(2)}) collective-permute-start(f32[16,256]{1,0:T(8,128)S(1)} %get-tuple-element.27), channel_id=1, source_target_pairs={{1,0},{2,1},{3,2},{4,3},{5,4},{6,5},{7,6},{8,7},{9,8},{10,9},{11,1... | collective-permute-start | bytes 49160 | tf_op jit(solution)/shard_map/ppermute | solution.py:20
  549.3 28.1 %collective-permute-start.7 = (f32[16,256]{1,0:T(8,128)S(1)}, f32[16,256]{1,0:T(8,128)S(1)}, u32[]{:S(2)}, u32[]{:S(2)}) collective-permute-start(f32[16,256]{1,0:T(8,128)S(1)} %get-tuple-element.28), channel_id=1, source_target_pairs={{0,1},{1,2},{2,3},{3,4},{4,5},{5,6},{6,7},{7,8},{8,9},{9,10},{10,1... | collective-permute-start | bytes 49160 | tf_op jit(solution)/shard_map/ppermute | solution.py:18
  553.2 25.3 %collective-permute-start.4 = (f32[4,6144]{1,0:T(4,128)S(1)}, f32[4,6144]{1,0:T(4,128)S(1)}, u32[]{:S(2)}, u32[]{:S(2)}) collective-permute-start(f32[4,6144]{1,0:T(4,128)S(1)} %get-tuple-element.25), channel_id=1, source_target_pairs={{16,0},{32,16},{48,32},{64,48},{80,64},{96,80},{112,96},{128,112},... | collective-permute-start | bytes 294920 | tf_op jit(solution)/shard_map/ppermute | solution.py:20
  574.1 6.3 %collective-permute-start.5 = (f32[4,6144]{1,0:T(4,128)S(1)}, f32[4,6144]{1,0:T(4,128)S(1)}, u32[]{:S(2)}, u32[]{:S(2)}) collective-permute-start(f32[4,6144]{1,0:T(4,128)S(1)} %get-tuple-element.26), channel_id=1, source_target_pairs={{0,16},{16,32},{32,48},{48,64},{64,80},{80,96},{96,112},{112,128},... | collective-permute-start | bytes 294920 | tf_op jit(solution)/shard_map/ppermute | solution.py:18
  582.4 19.5 %copy-start.8 = (f32[16,6144]{1,0:T(8,128)S(1)}, f32[16,6144]{1,0:T(8,128)}, u32[]{:S(2)}) copy-start(f32[16,6144]{1,0:T(8,128)} %squeeze_reshape.9) | copy-start | bytes 1179652
  582.4 19.5 %copy-start.9 = (f32[16,6144]{1,0:T(8,128)S(1)}, f32[16,6144]{1,0:T(8,128)}, u32[]{:S(2)}) copy-start(f32[16,6144]{1,0:T(8,128)} %squeeze_reshape.11) | copy-start | bytes 1179652
  582.4 19.5 %copy-start.10 = (f32[16,6144]{1,0:T(8,128)S(1)}, f32[16,6144]{1,0:T(8,128)}, u32[]{:S(2)}) copy-start(f32[16,6144]{1,0:T(8,128)} %squeeze_reshape.10) | copy-start | bytes 1179652
  583.0 16.3 %collective-permute-start.10 = (f32[16,256]{1,0:T(8,128)S(1)}, f32[16,256]{1,0:T(8,128)S(1)}, u32[]{:S(2)}, u32[]{:S(2)}) collective-permute-start(f32[16,256]{1,0:T(8,128)S(1)} %get-tuple-element.15), channel_id=1, source_target_pairs={{1,0},{2,1},{3,2},{4,3},{5,4},{6,5},{7,6},{8,7},{9,8},{10,9},{11,1... | collective-permute-start | bytes 49160 | tf_op jit(solution)/shard_map/ppermute | solution.py:20
  584.3 15.0 %collective-permute-start.11 = (f32[16,256]{1,0:T(8,128)S(1)}, f32[16,256]{1,0:T(8,128)S(1)}, u32[]{:S(2)}, u32[]{:S(2)}) collective-permute-start(f32[16,256]{1,0:T(8,128)S(1)} %get-tuple-element.16), channel_id=1, source_target_pairs={{0,1},{1,2},{2,3},{3,4},{4,5},{5,6},{6,7},{7,8},{8,9},{9,10},{10,1... | collective-permute-start | bytes 49160 | tf_op jit(solution)/shard_map/ppermute | solution.py:18
  588.3 12.0 %collective-permute-start.8 = (f32[4,6144]{1,0:T(4,128)S(1)}, f32[4,6144]{1,0:T(4,128)S(1)}, u32[]{:S(2)}, u32[]{:S(2)}) collective-permute-start(f32[4,6144]{1,0:T(4,128)S(1)} %get-tuple-element.13), channel_id=1, source_target_pairs={{16,0},{32,16},{48,32},{64,48},{80,64},{96,80},{112,96},{128,112},... | collective-permute-start | bytes 294920 | tf_op jit(solution)/shard_map/ppermute | solution.py:20
  590.2 11.7 %collective-permute-start.9 = (f32[4,6144]{1,0:T(4,128)S(1)}, f32[4,6144]{1,0:T(4,128)S(1)}, u32[]{:S(2)}, u32[]{:S(2)}) collective-permute-start(f32[4,6144]{1,0:T(4,128)S(1)} %get-tuple-element.14), channel_id=1, source_target_pairs={{0,16},{16,32},{32,48},{48,64},{64,80},{80,96},{96,112},{112,128},... | collective-permute-start | bytes 294920 | tf_op jit(solution)/shard_map/ppermute | solution.py:18
  (4 other events, 13.1 us)
where the time goes:
time: 615 us; the launch traced here: 605 us
  blocking collectives  489 us (80%)
  starting transfers between devices  63.7 us (10%)
  local copies, waits for them, and re-layouts  30.2 us (5%)
  matrix products  8.16 us (1%)
  other arithmetic  7.46 us (1%)
    all_gather x3, blocking collectives, expand(): lax.all_gather(blocks, 'gx', axis=1, tiled=True)  260 us
    all_gather x3, blocking collectives, expand(): lax.all_gather(partial_value, 'gy', axis=2, tiled=True)  229 us
    ppermute x6, starting transfers between devices, with_halo(): lax.ppermute(head, axis, [((i + 1) % count, i) for i in range(ends)])  35 us
    ppermute x6, starting transfers between devices, with_halo(): lax.ppermute(tail, axis, [(i, (i + 1) % count) for i in range(ends)])  28.8 us
  transfers between devices with their start and end apart: 12, of which 4 were waited for; matrix products, arithmetic and copies ran while one was open for 6% of the time, Pallas kernels for 0%

commit v1 on v0

v1 whole, which is shorter than its diff:
```python
import functools

import jax
import jax.numpy as jnp
import numpy as np
from jax import lax
from jax.experimental import pallas as pl
from jax.experimental.pallas import tpu as pltpu
from jax.sharding import PartitionSpec as P

STENCIL = (-205.0 / 72.0, 8.0 / 5.0, -1.0 / 5.0, 8.0 / 315.0, -1.0 / 560.0)
MESH = pl.DeviceIdType.MESH
F32, BF16 = jnp.float32, jnp.bfloat16

STEPS = 3
CX = 16
NZ = 64
YL = 96
TILES = YL * NZ // 128
POWER = 13.0
LIFT = 512.0


def constants():
    first = np.zeros((384, 768), np.float32)
    for core in range(2):
        for y in range(4):
            for zh in range(4):
                block = (y * 4 + zh) * 2 + core
                slot = (core * 4 + y) * 4 + zh
                for r in range(8):
                    first[block * 12 + r, slot * 8 + r] = 1.0
                for r in range(4):
                    first[block * 12 + 8 + r, 256 + slot * 8 + r] = 1.0
                    first[block * 12 + 8 + r, 512 + slot * 8 + 4 + r] = 1.0
    second = np.zeros((384, 384), np.float32)
    for block in range(16):
        for m in range(4):
            for q in range(6):
                second[block * 24 + 4 * q + m, block * 24 + 6 * m + q] = 1.0
    down = np.tile(np.eye(32, dtype=np.float32), (4, 1))
    across = np.tile(np.eye(64, dtype=np.float32), (1, 4))
    return tuple(jnp.asarray(a, BF16) for a in (first, second, down, across))


def dot(a, b):
    return lax.dot_general(a, b, (((1,), (0,)), ((), ())), preferred_element_type=F32)


def halves(a):
    high = a.astype(BF16)
    return high, (a - high.astype(F32)).astype(BF16)


def encode(value, scale):
    u = value * scale
    u2 = u * u
    u4 = u2 * u2
    return u4 * u4 * u4 * u


def decode(code, scale):
    size = jnp.abs(code)
    root = jnp.exp2(jnp.log2(jnp.maximum(size, 1e-38)) * (1.0 / POWER)) * scale
    root = jnp.where(size < 1e-37, 0.0, root)
    return jnp.where(code < 0.0, -root, root)


def kernel(
    pres, prev, vel, core, f1, f2, dep, pf1, pf2, down, across,
    out,
    pres_v, prev_v, vel_v, core_v, f1_v, f2_v, dep_v, pf1_v, pf2_v, down_v, across_v,
    kb, gb, fld, rolled, last, hxs, hxr, hys, hyr, v_s, w_s, g_s, t_s, bd_s, f1a_s, f1b_s, f2p_s,
    lsem, zs, zr, ys, yr, cs, cr, gzs, gzr, gxs, gxr, hxss, hxrs, hyss, hyrs,
):
    gx, gy = lax.axis_index("gx"), lax.axis_index("gy")
    y, zh, c = gx // 8, (gx // 2) % 4, gx % 2
    x, zl = gy // 4, gy % 4

    def at(y_, zh_, c_):
        return (y_ % 4) * 8 + (zh_ % 4) * 2 + c_

    def other(x_, zl_):
        return (x_ % 4) * 4 + zl_ % 4

    zpeer = [(at(y, zh + d, c), gy) for d in (1, 2, 3)]
    ypeer = [(at(y + d, zh, c), gy) for d in (1, 2, 3)]
    cpeer = (at(y, zh, 1 - c), gy)
    lpeer = [(gx, other(x, zl + d)) for d in (1, 2, 3)]
    xpeer = [(gx, other(x + d, zl)) for d in (1, 2, 3)]
    hx = [((gx + 31) % 32, gy), ((gx + 1) % 32, gy)]
    hy = [(gx, (gy + 15) % 16), (gx, (gy + 1) % 16)]

    barrier = pltpu.get_barrier_semaphore()
    everyone = zpeer + ypeer + [cpeer] + lpeer + xpeer + hx + hy
    for peer in everyone:
        pl.semaphore_signal(barrier, inc=1, device_id=peer, device_id_type=MESH)

    loads = [
        pltpu.make_async_copy(a, b, lsem.at[i])
        for i, (a, b) in enumerate(
            [
                (core, core_v), (pres, pres_v), (prev, prev_v), (vel, vel_v), (f1, f1_v), (pf1, pf1_v),
                (f2, f2_v), (pf2, pf2_v), (dep, dep_v), (down, down_v), (across, across_v),
            ]
        )
    ]
    for load in loads:
        load.start()

    def remote(src, dst, ssem, rsem, peer):
        return pltpu.make_async_remote_copy(
            src_ref=src, dst_ref=dst, send_sem=ssem, recv_sem=rsem, device_id=peer, device_id_type=MESH
        )

    sent = []

    def send(src, dst, ssem, rsem, peer):
        copy = remote(src, dst, ssem, rsem, peer)
        copy.start()
        sent.append(copy)

    def arrive(dst, ssem, rsem, peer):
        remote(dst, dst, ssem, rsem, peer).wait_recv()

    loads[0].wait()
    for s in range(STEPS):
        raw = core_v[s].astype(F32)
        tail = jnp.concatenate([raw[8:12, :384], raw[8:12, 384:]], axis=0)
        kb[s, c, y, zh] = jnp.concatenate([raw[:8], tail], axis=1).astype(BF16)

    pl.semaphore_wait(barrier, len(everyone))
    for s in range(STEPS):
        for d in range(3):
            own = kb.at[s, c, y, zh]
            send(own, own, zs.at[s, d], zr.at[s, d], zpeer[d])

    def pack_tile(level):
        def run(i, carry):
            for side, row in ((0, 8), (1, 20)):
                hxs[level, side, i, 0:4] = fld[level, 2 + i, row : row + 4]
                hxs[level, side, i, 4:8] = fld[level, 2 + TILES // 2 + i, row : row + 4]
            return carry

        lax.fori_loop(0, TILES // 2, run, 0, unroll=4)
        hys[level, 0] = fld[level, 2:4, 8:24]
        hys[level, 1] = fld[level, TILES : TILES + 2, 8:24]

    def send_halo(level):
        pack_tile(level)
        for side in (1, 0):
            send(hxs.at[level, side], hxr.at[level, 1 - side], hxss.at[level, side], hxrs.at[level, 1 - side], hx[side])
            send(hys.at[level, side], hyr.at[level, 1 - side], hyss.at[level, side], hyrs.at[level, 1 - side], hy[side])

    loads[1].wait()

    def spread(i, carry):
        fld[0, 2 + i, 8:24] = pres_v[:, pl.ds(pl.multiple_of(i * 128, 128), 128)]
        return carry

    lax.fori_loop(0, TILES, spread, 0, unroll=4)
    send_halo(0)

    for load in loads[4:]:
        load.wait()
    f1p = dot(f1_v[...], pf1_v[...]).astype(BF16)
    f1a_s[...] = f1p[:, :256]
    f1b_s[0:16] = f1p[:, 256:512]
    f1b_s[16:32] = f1p[:, 512:768]
    f2p_s[...] = dot(f2_v[...], pf2_v[...]).astype(BF16)
    tall = lax.dot_general(down_v[...], dep_v[...], (((1,), (1,)), ((), ())), preferred_element_type=F32)
    wide = dot(tall.astype(BF16), across_v[...])
    block_row = lax.broadcasted_iota(jnp.int32, (128, 256), 0) // 32
    block_col = lax.broadcasted_iota(jnp.int32, (128, 256), 1) // 64
    wide = jnp.where(block_row == block_col, wide, 0.0).astype(BF16)
    bd_s[0:128] = wide
    bd_s[128:256] = wide

    lane = lax.broadcasted_iota(jnp.int32, (CX, 128), 1)
    low_half = lane < 64
    level_z = lane % 64
    lane8 = lax.broadcasted_iota(jnp.int32, (8, 128), 1)

    def along_y(s):
        for d in range(3):
            slot = kb.at[s, c, y, (zh + 3 - d) % 4]
            arrive(slot, zs.at[s, d], zr.at[s, d], zpeer[d])
        row = kb.at[s, c, y]
        for d in range(3):
            send(row, row, ys.at[s, d], yr.at[s, d], ypeer[d])
        send(row, row, cs.at[s, 3], cr.at[s, 3], cpeer)

    def to_core(s):
        for d in range(3):
            row = kb.at[s, c, (y + 3 - d) % 4]
            arrive(row, ys.at[s, d], yr.at[s, d], ypeer[d])
            send(row, row, cs.at[s, d], cr.at[s, d], cpeer)

    def partial(s):
        arrive(kb.at[s, 1 - c, y], cs.at[s, 3], cr.at[s, 3], cpeer)
        for d in range(3):
            arrive(kb.at[s, 1 - c, (y + 3 - d) % 4], cs.at[s, d], cr.at[s, d], cpeer)
        blocks = kb[s].reshape(256, 1152)
        top = dot(f1a_s[...], blocks[:, :768])
        low = dot(f1b_s[...], blocks[:, 768:])
        value = top + jnp.concatenate([low[:16], low[16:]], axis=1)
        largest = jnp.max(jnp.abs(value), axis=(0, 1), keepdims=True)
        largest = jnp.maximum(largest * 1.01, 1e-30).astype(BF16).astype(F32)
        code = encode(value, LIFT / largest)
        for q in range(6):
            v_s[16 * q : 16 * q + 16] = code[:, 128 * q : 128 * q + 128]
        v_s[96:128] = jnp.zeros((32, 128), F32)
        rows = [v_s[pl.ds(i, 8, stride=16), :] for i in range(16)]
        for m in range(4):
            for j in range(4):
                chunk = None
                for t in range(4):
                    piece = rows[(t % 2) * 8 + 2 * j + t // 2]
                    shift = (32 * (t - m)) % 128
                    piece = pltpu.roll(piece, shift, 1) if shift else piece
                    chunk = piece if t == 0 else jnp.where(lane8 < 32 * t, chunk, piece)
                w_s[6 * m : 6 * m + 6, 128 * j : 128 * j + 128] = chunk[0:6]
        fold = jnp.concatenate([w_s[16:24, 0:256], w_s[16:24, 256:512]], axis=0)
        mark = jnp.broadcast_to(largest, (16, 128))
        gb[s, x, zl] = jnp.concatenate([w_s[0:16, :], fold, mark], axis=1).astype(BF16)
        own = gb.at[s, x, zl]
        for d in range(3):
            send(own, own, gzs.at[s, d], gzr.at[s, d], lpeer[d])

    def along_x(s):
        for d in range(3):
            arrive(gb.at[s, x, (zl + 3 - d) % 4], gzs.at[s, d], gzr.at[s, d], lpeer[d])
        row = gb.at[s, x]
        for d in range(3):
            send(row, row, gxs.at[s, d], gxr.at[s, d], xpeer[d])

    def step(t):
        for side in range(2):
            arrive(hxr.at[t, side], hxss.at[t, side], hxrs.at[t, side], hx[side])
            arrive(hyr.at[t, side], hyss.at[t, side], hyrs.at[t, side], hy[side])
        open_x = [gx > 0, gx < 31]
        open_y = [gy > 0, gy < 15]
        for side, first in ((0, 0), (1, TILES + 2)):
            fld[t, first : first + 2, 8:24] = jnp.where(open_y[side], hyr[t, side], 0.0)

        def place(i, carry):
            for side, row in ((0, 4), (1, 24)):
                got = jnp.where(open_x[side], hxr[t, side, i], 0.0)
                fld[t, 2 + i, row : row + 4] = got[0:4]
                fld[t, 2 + TILES // 2 + i, row : row + 4] = got[4:8]
            return carry

        lax.fori_loop(0, TILES // 2, place, 0, unroll=4)

        def turn(i, carry):
            rolled[i] = pltpu.roll(fld[t, i, 8:24], 64, 1)
            return carry

        lax.fori_loop(0, TILES + 4, turn, 0, unroll=4)

        def tile(i, carry):
            lanes = pl.ds(pl.multiple_of(i * 128, 128), 128)
            n = i + 2
            v = fld[t, n, 8:24]
            total = 3.0 * STENCIL[0] * v
            along = {
                1: rolled[n] + jnp.where(low_half, rolled[n - 1], rolled[n + 1]),
                2: fld[t, n - 1, 8:24] + fld[t, n + 1, 8:24],
                3: jnp.where(low_half, rolled[n + 1], rolled[n + 2]) + jnp.where(low_half, rolled[n - 2], rolled[n - 1]),
                4: fld[t, n - 2, 8:24] + fld[t, n + 2, 8:24],
            }
            for k in range(1, 5):
                near = along[k] + (fld[t, n, 8 - k : 24 - k] + fld[t, n, 8 + k : 24 + k])
                near = near + jnp.where(level_z + k < NZ, pltpu.roll(v, 128 - k, 1), 0.0)
                near = near + jnp.where(level_z >= k, pltpu.roll(v, k, 1), 0.0)
                total = total + STENCIL[k] * near
            before = prev_v[:, lanes] if t == 0 else fld[t - 1, n, 8:24]
            following = 2.0 * v - before + vel_v[:, lanes].astype(F32) * total
            if t < STEPS - 1:
                fld[t + 1, n, 8:24] = following
            else:
                last[i] = following
            return carry

        lax.fori_loop(0, TILES, tile, 0, unroll=2)
        if t < STEPS - 1:
            send_halo(t + 1)

    def finish(s):
        for d in range(3):
            arrive(gb.at[s, (x + 3 - d) % 4], gxs.at[s, d], gxr.at[s, d], xpeer[d])

        def block(b, carry):
            got = gb[s, b // 4, b % 4].astype(F32)
            scale = got[:, 768:896] * (1.0 / LIFT)
            value = jnp.concatenate(
                [decode(got[:, 128 * q : 128 * q + 128], scale) for q in range(6)], axis=1
            )
            start = pl.multiple_of(b * 24, 8)
            g_s[pl.ds(start, 16), :] = value[:, :512]
            g_s[pl.ds(pl.multiple_of(start + 16, 8), 8), :] = jnp.concatenate(
                [value[0:8, 512:768], value[8:16, 512:768]], axis=1
            )
            return carry

        lax.fori_loop(0, 16, block, 0)
        high, low = halves(g_s[...])
        mixed = dot(f2p_s[...], high) + dot(f2p_s[...], low)
        high, low = halves(mixed)
        for j in range(4):
            cols = slice(128 * j, 128 * j + 128)
            deep = dot(jnp.concatenate([high[:, cols], low[:, cols]], axis=1), bd_s[...])
            t_s[2 * j * YL : (2 * j + 1) * YL] = deep[:, :128]
            t_s[(2 * j + 1) * YL : (2 * j + 2) * YL] = deep[:, 128:]
        half8 = lane8 < 64

        def tile(i, carry):
            lanes = pl.ds(pl.multiple_of(i * 128, 128), 128)
            even = t_s[pl.ds(2 * i, 8, stride=YL), :]
            odd = t_s[pl.ds(2 * i + 1, 8, stride=YL), :]
            upper = jnp.where(half8, even, pltpu.roll(odd, 64, 1))
            lower = jnp.where(half8, pltpu.roll(even, 64, 1), odd)
            if s < STEPS - 1:
                following = fld[s + 1, i + 2, 8:24]
            else:
                following = last[i]
            term = jnp.concatenate([upper, lower], axis=0) * following
            out[:, lanes] = term if s == 0 else out[:, lanes] + term
            return carry

        lax.fori_loop(0, TILES, tile, 0, unroll=4)

    along_y(0)
    along_y(1)
    along_y(2)
    loads[2].wait()
    loads[3].wait()
    to_core(0)
    step(0)
    partial(0)
    to_core(1)
    partial(1)
    to_core(2)
    along_x(0)
    step(1)
    partial(2)
    along_x(1)
    finish(0)
    step(2)
    along_x(2)
    finish(1)
    finish(2)
    for copy in sent:
        copy.wait_send()


def body(pressure, previous, velocity, tucker_core, first_factor, second_factor, depth_factor):
    args = (pressure, previous, velocity, tucker_core, first_factor, second_factor, depth_factor) + constants()
    dma = pltpu.SemaphoreType.DMA
    return pl.pallas_call(
        kernel,
        out_shape=jax.ShapeDtypeStruct(pressure.shape, F32),
        in_specs=[pl.BlockSpec(memory_space=pl.ANY)] * len(args),
        out_specs=pl.BlockSpec(memory_space=pltpu.VMEM),
        scratch_shapes=[
            pltpu.VMEM(a.shape, a.dtype) for a in args
        ]
        + [
            pltpu.VMEM((STEPS, 2, 4, 4, 8, 1152), BF16),
            pltpu.VMEM((STEPS, 4, 4, 16, 896), BF16),
            pltpu.VMEM((STEPS, TILES + 4, 32, 128), F32),
            pltpu.VMEM((TILES + 4, CX, 128), F32),
            pltpu.VMEM((TILES, CX, 128), F32),
            pltpu.VMEM((STEPS, 2, TILES // 2, 8, 128), F32),
            pltpu.VMEM((STEPS, 2, TILES // 2, 8, 128), F32),
            pltpu.VMEM((STEPS, 2, 2, CX, 128), F32),
            pltpu.VMEM((STEPS, 2, 2, CX, 128), F32),
            pltpu.VMEM((128, 128), F32),
            pltpu.VMEM((24, 512), F32),
            pltpu.VMEM((384, 512), F32),
            pltpu.VMEM((8 * YL, 128), F32),
            pltpu.VMEM((256, 256), BF16),
            pltpu.VMEM((16, 256), BF16),
            pltpu.VMEM((32, 256), BF16),
            pltpu.VMEM((YL, 384), BF16),
            dma((len(args),)),
            dma((STEPS, 3)), dma((STEPS, 3)),
            dma((STEPS, 3)), dma((STEPS, 3)),
            dma((STEPS, 4)), dma((STEPS, 4)),
            dma((STEPS, 3)), dma((STEPS, 3)),
            dma((STEPS, 3)), dma((STEPS, 3)),
            dma((STEPS, 2)), dma((STEPS, 2)),
            dma((STEPS, 2)), dma((STEPS, 2)),
        ],
        compiler_params=pltpu.CompilerParams(
            collective_id=0, has_side_effects=True, vmem_limit_bytes=40 << 20
        ),
        name="image_steps",
    )(*args)


def solution(mesh):
    placed = (
        P("gx", "gy"),
        P("gx", "gy"),
        P("gx", "gy"),
        P(None, "gx", "gy"),
        P("gx", None),
        P("gy", None),
        P(),
    )
    return jax.shard_map(body, mesh=mesh, in_specs=placed, out_specs=P("gx", "gy"), check_vma=False)
```

time: 615 us -> 83.5 us (0.14); the launches traced: 605 us -> 83 us
  blocking collectives: 489 us -> 0 us
  Pallas kernels: 0 us -> 73.2 us
  starting transfers between devices: 63.7 us -> 0 us
  local copies, waits for them, and re-layouts: 30.2 us -> 9.77 us
  matrix products: 8.16 us -> 0 us
  other arithmetic: 7.46 us -> 0 us
    all_gather x6 -> x0, blocking collectives: 489 us -> none  [the longest x3 260 us: expand(): lax.all_gather(blocks, 'gx', axis=1, tiled=True)]
    pallas_call x0 -> x1, Pallas kernels: none -> 73.2 us  [body(): pl.pallas_call(kernel, out_shape=jax.ShapeDtypeStruct(pressure.shape, F32...]
    ppermute x12 -> x0, starting transfers between devices: 63.7 us -> none  [the longest x6 35 us: with_halo(): lax.ppermute(head, axis, [((i + 1) % count, i) for i in range(ends)])]
    all_gather x6 -> x0, local copies, waits for them, and re-layouts: 12.7 us -> none  [the longest x3 6.98 us: expand(): lax.all_gather(partial_value, 'gy', axis=2, tiled=True)]
    slice x22 -> x0, local copies, waits for them, and re-layouts: 11.9 us -> none  [the longest x12 7.68 us: laplace(): deeper = jnp.concatenate([field[:, reach:], blank[:, :reach]], axis=1)]
    unnamed x34 -> x22, local copies, waits for them, and re-layouts: 0.87 us -> 9.77 us
    dot_general x9 -> x0, matrix products: 8.16 us -> none  [the longest x3 4.28 us: expand(): jnp.einsum('xr,srnc->sxnc', columns, lax.all_gather(blocks, 'gx', axis=1,...]
    add x3 -> x0, other arithmetic: 7.41 us -> none  [the longest x2 4.74 us: body(): following = 2.0 * current - before + speed * laplace(current, depth_cells)]
  transfers between devices with their start and end apart: 12 -> 0, of which waited for: 4 -> 0; matrix products, arithmetic and copies ran while one was open for 6% -> 0% of each run, Pallas kernels for 0% -> 0%
where the time goes in v1:
time: 83.5 us; the launch traced here: 83 us
  Pallas kernels  73.2 us (88%)
  local copies, waits for them, and re-layouts  9.77 us (12%)
    pallas_call x1, Pallas kernels, body(): pl.pallas_call(kernel, out_shape=jax.ShapeDtypeStruct(pressure.shape, F32...  73.2 us
    unnamed x22, local copies, waits for them, and re-layouts  9.77 us

profile of v1, /device:TPU:1, one launch (start us, length us, event | category | flops | bytes accessed | tf_op | source)
XLA Modules:
  0.0 83.0 jit_solution(18385858530888480885)
XLA Ops:
  0.0 0.0 copy-start.9
  0.0 0.8 copy.12.dep
  0.8 0.0 copy-done.9
  0.8 0.0 copy-start
  0.8 1.1 %copy-done = bf16[384,768]{1,0:T(8,128)(2,1)S(1)} copy-done((bf16[384,768]{1,0:T(8,128)(2,1)S(1)}, bf16[384,768]{1,0:T(8,128)(2,1)}, u32[]{:S(2)}) %copy-start) | copy-done | bytes 589848
  1.9 0.0 copy-start.1
  1.9 1.0 %copy-done.1 = f32[16,6144]{1,0:T(8,128)S(1)} copy-done((f32[16,6144]{1,0:T(8,128)S(1)}, f32[16,6144]{1,0:T(8,128)}, u32[]{:S(2)}) %copy-start.1) | copy-done | bytes 393240
  2.9 0.0 copy-start.2
  2.9 1.0 %copy-done.2 = f32[16,6144]{1,0:T(8,128)S(1)} copy-done((f32[16,6144]{1,0:T(8,128)S(1)}, f32[16,6144]{1,0:T(8,128)}, u32[]{:S(2)}) %copy-start.2) | copy-done | bytes 393240
  3.9 0.0 copy-start.3
  3.9 1.0 %copy-done.3 = bf16[384,384]{1,0:T(8,128)(2,1)S(1)} copy-done((bf16[384,384]{1,0:T(8,128)(2,1)S(1)}, bf16[384,384]{1,0:T(8,128)(2,1)}, u32[]{:S(2)}) %copy-start.3) | copy-done | bytes 294936
  4.8 0.0 copy-start.4
  4.8 0.9 %copy-done.4 = bf16[16,6144]{1,0:T(8,128)(2,1)S(1)} copy-done((bf16[16,6144]{1,0:T(8,128)(2,1)S(1)}, bf16[16,6144]{1,0:T(8,128)(2,1)}, u32[]{:S(2)}) %copy-start.4) | copy-done | bytes 196632
  5.8 0.0 copy-start.5
  5.8 0.9 %copy-done.5 = bf16[3,12,768]{2,1,0:T(8,128)(2,1)S(1)} copy-done((bf16[3,12,768]{2,1,0:T(8,128)(2,1)S(1)}, bf16[3,12,768]{2,1,0:T(8,128)(2,1)}, u32[]{:S(2)}) %copy-start.5) | copy-done | bytes 55320
  6.6 0.0 copy-start.6
  6.6 0.9 %copy-done.6 = bf16[96,384]{1,0:T(8,128)(2,1)S(1)} copy-done((bf16[96,384]{1,0:T(8,128)(2,1)S(1)}, bf16[96,384]{1,0:T(8,128)(2,1)}, u32[]{:S(2)}) %copy-start.6) | copy-done | bytes 73752
  7.5 0.0 copy-start.7
  7.5 0.8 copy-done.7
  8.3 0.0 copy-start.8
  8.3 0.8 copy-done.8
  9.0 73.2 %image_steps.1 = f32[16,6144]{1,0:T(8,128)S(1)} custom-call(f32[16,6144]{1,0:T(8,128)S(1)} %copy-done.1, f32[16,6144]{1,0:T(8,128)S(1)} %copy-done.2, bf16[16,6144]{1,0:T(8,128)(2,1)S(1)} %copy-done.4, bf16[3,12,768]{2,1,0:T(8,128)(2,1)S(1)} %copy-done.5, bf16[16,384]{1,0:T(8,128)(2,1)S(1)} %copy-done.9, bf16[96,384]{1,0:T(8,128)(2,1)S(1)} %copy-done.6, ...), custom_call_target="tpu_custom_call" | custom-call | tf_op jit(solution)/shard_map/image_steps/pallas_call | solution.py:360
  82.2 0.7 copy.14
Async XLA Ops:
  0.0 0.8 copy-start.9
  0.8 1.1 %copy-start = (bf16[384,768]{1,0:T(8,128)(2,1)S(1)}, bf16[384,768]{1,0:T(8,128)(2,1)}, u32[]{:S(2)}) copy-start(bf16[384,768]{1,0:T(8,128)(2,1)} %constant.8.clone.pf1) | copy-start | bytes 1769476
  1.9 1.0 %copy-start.1 = (f32[16,6144]{1,0:T(8,128)S(1)}, f32[16,6144]{1,0:T(8,128)}, u32[]{:S(2)}) copy-start(f32[16,6144]{1,0:T(8,128)} %pres.1) | copy-start | bytes 1179652
  2.9 1.0 %copy-start.2 = (f32[16,6144]{1,0:T(8,128)S(1)}, f32[16,6144]{1,0:T(8,128)}, u32[]{:S(2)}) copy-start(f32[16,6144]{1,0:T(8,128)} %prev.1) | copy-start | bytes 1179652
  3.9 1.0 %copy-start.3 = (bf16[384,384]{1,0:T(8,128)(2,1)S(1)}, bf16[384,384]{1,0:T(8,128)(2,1)}, u32[]{:S(2)}) copy-start(bf16[384,384]{1,0:T(8,128)(2,1)} %constant.9.clone.pf2) | copy-start | bytes 884740
  4.8 0.9 %copy-start.4 = (bf16[16,6144]{1,0:T(8,128)(2,1)S(1)}, bf16[16,6144]{1,0:T(8,128)(2,1)}, u32[]{:S(2)}) copy-start(bf16[16,6144]{1,0:T(8,128)(2,1)} %vel.1) | copy-start | bytes 589828
  5.8 0.9 %copy-start.5 = (bf16[3,12,768]{2,1,0:T(8,128)(2,1)S(1)}, bf16[3,12,768]{2,1,0:T(8,128)(2,1)}, u32[]{:S(2)}) copy-start(bf16[3,12,768]{2,1,0:T(8,128)(2,1)} %core.1) | copy-start | bytes 165892
  6.6 0.9 %copy-start.6 = (bf16[96,384]{1,0:T(8,128)(2,1)S(1)}, bf16[96,384]{1,0:T(8,128)(2,1)}, u32[]{:S(2)}) copy-start(bf16[96,384]{1,0:T(8,128)(2,1)} %f2.1) | copy-start | bytes 221188
  7.5 0.8 copy-start.7
  8.3 0.8 copy-start.8

commit v2 on v1

v2 whole, which is shorter than its diff:
```python
import functools

import jax
import jax.numpy as jnp
import numpy as np
from jax import lax
from jax.experimental import pallas as pl
from jax.experimental.pallas import tpu as pltpu
from jax.sharding import PartitionSpec as P

STENCIL = (-205.0 / 72.0, 8.0 / 5.0, -1.0 / 5.0, 8.0 / 315.0, -1.0 / 560.0)
MESH = pl.DeviceIdType.MESH
F32, BF16 = jnp.float32, jnp.bfloat16

STEPS = 3
CX = 16
NZ = 64
YL = 96
TILES = YL * NZ // 128
POWER = 13.0
LIFT = 512.0


def constants():
    first = np.zeros((384, 768), np.float32)
    for core in range(2):
        for y in range(4):
            for zh in range(4):
                block = (y * 4 + zh) * 2 + core
                slot = (core * 4 + y) * 4 + zh
                for r in range(8):
                    first[block * 12 + r, slot * 8 + r] = 1.0
                for r in range(4):
                    first[block * 12 + 8 + r, 256 + slot * 8 + r] = 1.0
                    first[block * 12 + 8 + r, 512 + slot * 8 + 4 + r] = 1.0
    second = np.zeros((384, 384), np.float32)
    for block in range(16):
        for m in range(4):
            for q in range(6):
                second[block * 24 + 4 * q + m, block * 24 + 6 * m + q] = 1.0
    down = np.tile(np.eye(32, dtype=np.float32), (4, 1))
    across = np.tile(np.eye(64, dtype=np.float32), (1, 4))
    z = np.arange(128)
    lines = np.zeros((128, 128), np.float64)
    for k in range(1, 5):
        near = np.abs(z[:, None] - z[None, :]) == k
        lines += STENCIL[k] * (near & (z[:, None] // 64 == z[None, :] // 64))
    swap = (np.abs(z[:, None] - z[None, :]) == 64).astype(np.float64)
    lines += STENCIL[1] * swap
    high = lines.astype(BF16)
    low = (lines - high.astype(np.float64)).astype(BF16)
    top = np.concatenate([high, swap.astype(BF16)], axis=1)
    near_z = np.concatenate([top, top, np.concatenate([low, np.zeros((128, 128), BF16)], axis=1)], axis=0)
    return tuple(jnp.asarray(a, BF16) for a in (first, second, down, across, near_z))


def dot(a, b):
    return lax.dot_general(a, b, (((1,), (0,)), ((), ())), preferred_element_type=F32)


def halves(a):
    high = a.astype(BF16)
    return high, (a - high.astype(F32)).astype(BF16)


def encode(value, scale):
    u = value * scale
    u2 = u * u
    u4 = u2 * u2
    return u4 * u4 * u4 * u


def decode(code, scale):
    size = jnp.abs(code)
    root = jnp.exp2(jnp.log2(jnp.maximum(size, 1e-38)) * (1.0 / POWER)) * scale
    root = jnp.where(size < 1e-37, 0.0, root)
    return jnp.where(code < 0.0, -root, root)


def place(x, r):
    return ((x + 4) * 10 + r + 2) * 8


def kernel(
    pres, prev, vel, core, f1, f2, dep, pf1, pf2, down, across, near_z,
    out,
    pres_v, prev_v, vel_v, core_v, f1_v, f2_v, dep_v, pf1_v, pf2_v, down_v, across_v, near_z_v,
    kb, gb, fld, swapped, deep_z, speed, last, image, hxs, hxr, hys, hyr, v_s, w_s, g_s, t_s, bd_s, f1a_s, f1b_s, f2p_s,
    lsem, zs, zr, ys, yr, cs, cr, gzs, gzr, gxs, gxr, hxss, hxrs, hyss, hyrs,
):
    gx, gy = lax.axis_index("gx"), lax.axis_index("gy")
    y, zh, c = gx // 8, (gx // 2) % 4, gx % 2
    x, zl = gy // 4, gy % 4

    def at(y_, zh_, c_):
        return ((y_ % 4) * 8 + (zh_ % 4) * 2 + c_, gy)

    def other(x_, zl_):
        return (gx, (x_ % 4) * 4 + zl_ % 4)

    zpeer = [at(y, zh + d, c) for d in (1, 2, 3)]
    ypeer = [at(y + d, zh, c) for d in (1, 2, 3)]
    cpeer = at(y, zh, 1 - c)
    lpeer = [other(x, zl + d) for d in (1, 2, 3)]
    xpeer = [other(x + 1, zl), other(x + 3, zl)]
    hx = [((gx + 31) % 32, gy), ((gx + 1) % 32, gy)]
    hy = [(gx, (gy + 15) % 16), (gx, (gy + 1) % 16)]

    barrier = pltpu.get_barrier_semaphore()
    everyone = zpeer + ypeer + [cpeer] + lpeer + xpeer + hx + hy
    for peer in everyone:
        pl.semaphore_signal(barrier, inc=1, device_id=peer, device_id_type=MESH)

    loads = [
        pltpu.make_async_copy(a, b, lsem.at[i])
        for i, (a, b) in enumerate(
            [
                (core, core_v), (pres, pres_v), (prev, prev_v), (vel, vel_v), (f1, f1_v), (pf1, pf1_v),
                (f2, f2_v), (pf2, pf2_v), (dep, dep_v), (down, down_v), (across, across_v), (near_z, near_z_v),
            ]
        )
    ]
    for load in loads:
        load.start()

    def remote(src, dst, ssem, rsem, peer):
        return pltpu.make_async_remote_copy(
            src_ref=src, dst_ref=dst, send_sem=ssem, recv_sem=rsem, device_id=peer, device_id_type=MESH
        )

    sent = []

    def send(src, dst, ssem, rsem, peer):
        copy = remote(src, dst, ssem, rsem, peer)
        copy.start()
        sent.append(copy)

    def arrive(dst, ssem, rsem, peer):
        remote(dst, dst, ssem, rsem, peer).wait_recv()

    def flush(count=None):
        for _ in range(len(sent) if count is None else count):
            sent.pop(0).wait_send()

    loads[0].wait()
    for s in range(STEPS):
        raw = core_v[s].astype(F32)
        tail = jnp.concatenate([raw[8:12, :384], raw[8:12, 384:]], axis=0)
        kb[s, c, y, zh] = jnp.concatenate([raw[:8], tail], axis=1).astype(BF16)

    def along_z(s):
        own = kb.at[s, c, y, zh]
        for k in range(3):
            to = k + jnp.where(k >= zh, 1, 0)
            send(own, own, zs.at[s, k], zr.at[s, zh], at(y, to, c))

    def along_y(s):
        for d in range(3):
            source = (zh + 3 - d) % 4
            arrive(kb.at[s, c, y, source], zs.at[s, d], zr.at[s, source], zpeer[d])
        row = kb.at[s, c, y]
        for d in (0, 2, 1):
            send(row, row, ys.at[s, d], yr.at[s, d], ypeer[d])
        send(row, row, cs.at[s, 3], cr.at[s, 3], cpeer)

    def to_core(s):
        for d in (0, 2, 1):
            row = kb.at[s, c, (y + 3 - d) % 4]
            arrive(row, ys.at[s, d], yr.at[s, d], ypeer[d])
            send(row, row, cs.at[s, d], cr.at[s, d], cpeer)

    low_half = lax.broadcasted_iota(jnp.int32, (8, 128), 1) < 64
    sub = lax.broadcasted_iota(jnp.int32, (8, 128), 0)

    def rows(start, count=8):
        return pl.ds(pl.multiple_of(start, 8), count)

    def strided(x_, r):
        return pl.ds((x_ // 8) * 384 + r * 8 + x_ % 8, 8, stride=48)

    def send_halo(t):
        for side in range(2):
            for k in range(4):
                layer = k if side == 0 else 12 + k
                outer = k == 0 if side == 0 else k == 3
                for p in range(3):
                    pair = fld[t, rows(place(layer, 2 * p), 16), :]
                    high = pair.astype(BF16)
                    hxs[t, side, k, p] = high
                    if outer:
                        hxs[t, side, 4, p] = (pair - high.astype(F32)).astype(BF16)
        for side in range(2):
            for i in range(2):
                for half in range(2):
                    start = place(8 * half, i) if side == 0 else place(8 * half, 4 + i) + 7
                    hys[t, side, i, 8 * half : 8 * half + 8] = fld[t, pl.ds(start, 8, stride=80), :]
        for side in (1, 0):
            send(hxs.at[t, side], hxr.at[t, 1 - side], hxss.at[t, side], hxrs.at[t, 1 - side], hx[side])
            send(hys.at[t, side], hyr.at[t, 1 - side], hyss.at[t, side], hyrs.at[t, 1 - side], hy[side])

    def inner(t):
        def run(q, carry):
            cells = jnp.concatenate([fld[t, rows(place(4 * q + k, 0), 48), :] for k in range(4)], axis=0)
            high, low = halves(cells)
            both = dot(jnp.concatenate([high, low], axis=1), near_z_v[0:256])
            along = both[:, :128] + dot(high, near_z_v[256:384, :128])
            for k in range(4):
                deep_z[rows((4 * q + k) * 48, 48), :] = along[48 * k : 48 * k + 48]
                swapped[rows(place(4 * q + k, 0), 48), :] = both[48 * k : 48 * k + 48, 128:]
            return carry

        lax.fori_loop(0, 4, run, 0)

    def step(t):
        for side in range(2):
            arrive(hyr.at[t, side], hyss.at[t, side], hyrs.at[t, side], hy[side])
        open_y = [gy > 0, gy < 15]
        edges = ((-2, 4, 0, 0, 1), (-1, 5, 0, 1, 1), (6, 0, 1, 0, 7), (7, 1, 1, 1, 7))
        for _, _, side, i, _ in edges:
            hyr[t, side, i] = jnp.where(open_y[side], hyr[t, side, i], 0.0)

        def edge(x_, carry):
            for r, source, side, i, turn in edges:
                halo = hyr[t, side, i, pl.ds(x_, 1), :]
                here = sub == (0 if side == 0 else 7)
                moved = pltpu.roll(fld[t, rows(place(x_, source)), :], turn, 0)
                fld[t, rows(place(x_, r)), :] = jnp.where(here, halo, moved)
                moved = pltpu.roll(swapped[rows(place(x_, source)), :], turn, 0)
                swapped[rows(place(x_, r)), :] = jnp.where(here, pltpu.roll(halo, 64, 1), moved)
            return carry

        lax.fori_loop(0, CX, edge, 0, unroll=2)
        for side in range(2):
            arrive(hxr.at[t, side], hxss.at[t, side], hxrs.at[t, side], hx[side])
        open_x = [gx > 0, gx < 31]
        for side in range(2):
            for k in range(4):
                layer = k - 4 if side == 0 else 16 + k
                outer = k == 3 if side == 0 else k == 0
                for p in range(3):
                    pair = hxr[t, side, k, p].astype(F32)
                    if outer:
                        pair = pair + hxr[t, side, 4, p].astype(F32)
                    fld[t, rows(place(layer, 2 * p), 16), :] = jnp.where(open_x[side], pair, 0.0)

        def line(x_, carry):
            v = {r: fld[t, rows(place(x_, r)), :] for r in range(-2, 8)}
            w = {r: swapped[rows(place(x_, r)), :] for r in range(-2, 8)}
            for r in range(6):
                along = {
                    1: jnp.where(low_half, w[r - 1], w[r + 1]),
                    2: v[r - 1] + v[r + 1],
                    3: jnp.where(low_half, w[r + 1], w[r + 2]) + jnp.where(low_half, w[r - 2], w[r - 1]),
                    4: v[r - 2] + v[r + 2],
                }
                total = deep_z[rows((x_ * 6 + r) * 8), :] + (3.0 * STENCIL[0]) * v[r]
                for k in range(1, 5):
                    near = fld[t, rows(place(x_ - k, r)), :] + fld[t, rows(place(x_ + k, r)), :]
                    total = total + STENCIL[k] * (near + along[k])
                if t == 0:
                    before = prev_v[strided(x_, r), :]
                else:
                    before = fld[t - 1, rows(place(x_, r)), :]
                following = 2.0 * v[r] - before + speed[rows((x_ * 6 + r) * 8), :] * total
                if t < STEPS - 1:
                    fld[t + 1, rows(place(x_, r)), :] = following
                else:
                    last[rows((x_ * 6 + r) * 8), :] = following
            return carry

        lax.fori_loop(0, CX, line, 0)
        if t < STEPS - 1:
            send_halo(t + 1)
            inner(t + 1)

    lane8 = lax.broadcasted_iota(jnp.int32, (8, 128), 1)

    def partial(s):
        arrive(kb.at[s, 1 - c, y], cs.at[s, 3], cr.at[s, 3], cpeer)
        for d in range(3):
            arrive(kb.at[s, 1 - c, (y + 3 - d) % 4], cs.at[s, d], cr.at[s, d], cpeer)
        blocks = kb[s].reshape(256, 1152)
        top = dot(f1a_s[...], blocks[:, :768])
        low = dot(f1b_s[...], blocks[:, 768:])
        value = top + jnp.concatenate([low[:16], low[16:]], axis=1)
        largest = jnp.max(jnp.abs(value), axis=(0, 1), keepdims=True)
        largest = jnp.maximum(largest * 1.01, 1e-30).astype(BF16).astype(F32)
        code = encode(value, LIFT / largest)
        for q in range(6):
            v_s[16 * q : 16 * q + 16] = code[:, 128 * q : 128 * q + 128]
        v_s[96:128] = jnp.zeros((32, 128), F32)
        lines = [v_s[pl.ds(i, 8, stride=16), :] for i in range(16)]
        for m in range(4):
            for j in range(4):
                chunk = None
                for t in range(4):
                    piece = lines[(t % 2) * 8 + 2 * j + t // 2]
                    shift = (32 * (t - m)) % 128
                    piece = pltpu.roll(piece, shift, 1) if shift else piece
                    chunk = piece if t == 0 else jnp.where(lane8 < 32 * t, chunk, piece)
                w_s[6 * m : 6 * m + 6, 128 * j : 128 * j + 128] = chunk[0:6]
        fold = jnp.concatenate([w_s[16:24, 0:256], w_s[16:24, 256:512]], axis=0)
        mark = jnp.broadcast_to(largest, (16, 128))
        gb[s, x, zl] = jnp.concatenate([w_s[0:16, :], fold, mark], axis=1).astype(BF16)
        own = gb.at[s, x, zl]
        for d in range(3):
            send(own, own, gzs.at[s, d], gzr.at[s, d], lpeer[d])

    def decode_row(s, row):
        def block(b, carry):
            got = gb[s, row, b].astype(F32)
            scale = got[:, 768:896] * (1.0 / LIFT)
            value = jnp.concatenate([decode(got[:, 128 * q : 128 * q + 128], scale) for q in range(6)], axis=1)
            start = (row * 4 + b) * 24
            g_s[s, rows(start, 16), :] = value[:, :512]
            g_s[s, rows(start + 16), :] = jnp.concatenate([value[0:8, 512:768], value[8:16, 512:768]], axis=1)
            return carry

        lax.fori_loop(0, 4, block, 0)

    def start_x(s):
        for d in range(3):
            arrive(gb.at[s, x, (zl + 3 - d) % 4], gzs.at[s, d], gzr.at[s, d], lpeer[d])
        row = gb.at[s, x]
        for side in range(2):
            send(row, row, gxs.at[s, side], gxr.at[s, side], xpeer[side])
        decode_row(s, x)

    def forward_x(s):
        for side in range(2):
            source = (x + 3 - 2 * side) % 4
            arrive(gb.at[s, source], gxs.at[s, side], gxr.at[s, side], xpeer[side])
            half = gb.at[s, source, pl.ds(2 * side, 2)]
            send(half, half, gxs.at[s, 2 + side], gxr.at[s, 2 + side], xpeer[side])
        for side in range(2):
            decode_row(s, (x + 3 - 2 * side) % 4)

    def finish(s):
        for side in range(2):
            half = gb.at[s, (x + 2) % 4, pl.ds(2 * side, 2)]
            arrive(half, gxs.at[s, 2 + side], gxr.at[s, 2 + side], xpeer[side])
        decode_row(s, (x + 2) % 4)
        high, low = halves(g_s[s])
        mixed = dot(f2p_s[...], high) + dot(f2p_s[...], low)
        high, low = halves(mixed)
        for j in range(4):
            cols = slice(128 * j, 128 * j + 128)
            deep = dot(jnp.concatenate([high[:, cols], low[:, cols]], axis=1), bd_s[...])
            for i in range(4):
                start = (i // 2) * 8 * YL + (2 * j + i % 2) * YL
                t_s[start : start + YL] = deep[:, 128 * i : 128 * i + 128]

        def line(j, carry):
            for r in range(6):
                even, odd, even_turned, odd_turned = (
                    t_s[pl.ds(j * YL + 2 * r + offset, 8, stride=12), :] for offset in (0, 1, 8 * YL, 8 * YL + 1)
                )
                for x2, term in (
                    (0, jnp.where(low_half, even, odd_turned)),
                    (1, jnp.where(low_half, even_turned, odd)),
                ):
                    x_ = x2 * 8 + j
                    here = rows((x_ * 6 + r) * 8)
                    if s < STEPS - 1:
                        term = term * fld[s + 1, rows(place(x_, r)), :]
                    else:
                        term = term * last[here, :]
                    if s > 0:
                        term = term + image[here, :]
                    if s < STEPS - 1:
                        image[here, :] = term
                    else:
                        out[strided(x_, r), :] = term
            return carry

        lax.fori_loop(0, 8, line, 0)

    def prepare():
        for load in loads[4:11]:
            load.wait()
        f1p = dot(f1_v[...], pf1_v[...]).astype(BF16)
        f1a_s[...] = f1p[:, :256]
        f1b_s[0:16] = f1p[:, 256:512]
        f1b_s[16:32] = f1p[:, 512:768]
        f2p_s[...] = dot(f2_v[...], pf2_v[...]).astype(BF16)
        tall = dot(down_v[...], dep_v[...])
        wide = dot(tall.astype(BF16), across_v[...])
        block_row = lax.broadcasted_iota(jnp.int32, (128, 256), 0) // 32
        block_col = lax.broadcasted_iota(jnp.int32, (128, 256), 1) // 64
        swap_col = block_col + 1 - 2 * (block_col % 2)
        for i, col in enumerate((block_col, swap_col)):
            part = jnp.where(block_row == col, wide, 0.0).astype(BF16)
            bd_s[0:128, 256 * i : 256 * i + 256] = part
            bd_s[128:256, 256 * i : 256 * i + 256] = part

    def first_fields():
        loads[1].wait()

        def spread(xs, carry):
            for xt in range(2):
                for r in range(6):
                    fld[0, rows(place(xt * 8 + xs, r)), :] = pres_v[pl.ds(xt * 384 + r * 8 + xs, 8, stride=48), :]
            return carry

        lax.fori_loop(0, 8, spread, 0)

    def speeds():
        loads[3].wait()
        last[...] = vel_v[...].astype(F32)

        def spread(xs, carry):
            for xt in range(2):
                for r in range(6):
                    speed[rows(((xt * 8 + xs) * 6 + r) * 8), :] = last[pl.ds(xt * 384 + r * 8 + xs, 8, stride=48), :]
            return carry

        lax.fori_loop(0, 8, spread, 0)
        loads[2].wait()

    pl.semaphore_wait(barrier, len(everyone))
    along_z(0)
    first_fields()
    send_halo(0)
    flush(3)
    along_z(1)
    prepare()
    loads[11].wait()
    inner(0)
    flush(4)
    flush(3)
    along_z(2)
    speeds()
    along_y(0)
    along_y(1)
    to_core(0)
    step(0)
    along_y(2)
    partial(0)
    to_core(1)
    partial(1)
    start_x(0)
    to_core(2)
    partial(2)
    start_x(1)
    forward_x(0)
    step(1)
    start_x(2)
    forward_x(1)
    finish(0)
    forward_x(2)
    step(2)
    finish(1)
    finish(2)
    flush()


def tiles(a):
    return a.reshape(2, 8, TILES, 128).transpose(0, 2, 1, 3).reshape(CX * TILES, 128)


def body(pressure, previous, velocity, tucker_core, first_factor, second_factor, depth_factor):
    args = (tiles(pressure), tiles(previous), tiles(velocity), tucker_core, first_factor, second_factor, depth_factor.T)
    args = args + constants()
    dma = pltpu.SemaphoreType.DMA
    image = pl.pallas_call(
        kernel,
        out_shape=jax.ShapeDtypeStruct((CX * TILES, 128), F32),
        in_specs=[pl.BlockSpec(memory_space=pl.ANY)] * len(args),
        out_specs=pl.BlockSpec(memory_space=pltpu.VMEM),
        scratch_shapes=[
            pltpu.VMEM(a.shape, a.dtype) for a in args
        ]
        + [
            pltpu.VMEM((STEPS, 2, 4, 4, 8, 1152), BF16),
            pltpu.VMEM((STEPS, 4, 4, 16, 896), BF16),
            pltpu.VMEM((STEPS, 24 * 10 * 8, 128), F32),
            pltpu.VMEM((24 * 10 * 8, 128), F32),
            pltpu.VMEM((CX * TILES, 128), F32),
            pltpu.VMEM((CX * TILES, 128), F32),
            pltpu.VMEM((CX * TILES, 128), F32),
            pltpu.VMEM((CX * TILES, 128), F32),
            pltpu.VMEM((STEPS, 2, 5, 3, 16, 128), BF16),
            pltpu.VMEM((STEPS, 2, 5, 3, 16, 128), BF16),
            pltpu.VMEM((STEPS, 2, 2, CX, 128), F32),
            pltpu.VMEM((STEPS, 2, 2, CX, 128), F32),
            pltpu.VMEM((128, 128), F32),
            pltpu.VMEM((24, 512), F32),
            pltpu.VMEM((STEPS, 384, 512), F32),
            pltpu.VMEM((2 * 8 * YL, 128), F32),
            pltpu.VMEM((256, 512), BF16),
            pltpu.VMEM((16, 256), BF16),
            pltpu.VMEM((32, 256), BF16),
            pltpu.VMEM((YL, 384), BF16),
            dma((len(args),)),
            dma((STEPS, 3)), dma((STEPS, 4)),
            dma((STEPS, 3)), dma((STEPS, 3)),
            dma((STEPS, 4)), dma((STEPS, 4)),
            dma((STEPS, 3)), dma((STEPS, 3)),
            dma((STEPS, 4)), dma((STEPS, 4)),
            dma((STEPS, 2)), dma((STEPS, 2)),
            dma((STEPS, 2)), dma((STEPS, 2)),
        ],
        compiler_params=pltpu.CompilerParams(
            collective_id=0, has_side_effects=True, vmem_limit_bytes=60 << 20
        ),
        name="image_steps",
    )(*args)
    return image.reshape(2, TILES, 8, 128).transpose(0, 2, 1, 3).reshape(CX, 8 * TILES * 16)


def solution(mesh):
    placed = (
        P("gx", "gy"),
        P("gx", "gy"),
        P("gx", "gy"),
        P(None, "gx", "gy"),
        P("gx", None),
        P("gy", None),
        P(),
    )
    return jax.shard_map(body, mesh=mesh, in_specs=placed, out_specs=P("gx", "gy"), check_vma=False)
```

time: 83.5 us -> 62.9 us (0.75)
  Pallas kernels: 73.2 us -> 60.9 us
  local copies, waits for them, and re-layouts: 9.77 us -> 1.77 us
    pallas_call x1, Pallas kernels: 73.2 us -> 60.9 us  [body(): pl.pallas_call(kernel, out_shape=jax.ShapeDtypeStruct((CX * TILES, 128),...]
    unnamed x22 -> x1, local copies, waits for them, and re-layouts: 9.77 us -> 1.77 us
where the time goes in v2:
time: 62.9 us; the launch traced here: 62.7 us
  Pallas kernels  60.9 us (97%)
  local copies, waits for them, and re-layouts  1.77 us (3%)
    pallas_call x1, Pallas kernels, body(): pl.pallas_call(kernel, out_shape=jax.ShapeDtypeStruct((CX * TILES, 128),...  60.9 us
    unnamed x1, local copies, waits for them, and re-layouts  1.77 us

profile of v2, /device:TPU:1, one launch (start us, length us, event | category | flops | bytes accessed | tf_op | source)
XLA Modules:
  0.0 62.7 jit_solution(3281878297258420662)
XLA Ops:
  0.0 60.9 %image_steps.1 = f32[768,128]{1,0:T(8,128)} custom-call(f32[768,128]{1,0:T(8,128)} %bitcast.22, f32[768,128]{1,0:T(8,128)} %bitcast.23, bf16[768,128]{1,0:T(8,128)(2,1)} %bitcast.24, bf16[3,12,768]{2,1,0:T(8,128)(2,1)} %core.1, bf16[16,384]{1,0:T(8,128)(2,1)} %f1.1, bf16[96,384]{1,0:T(8,128)(2,1)} %f2.1, bf16[32,64]{1,0:T(8,128)(2,1)} %bitcast.25, ...), custom_call_target="tpu_custom_call" | custom-call | tf_op jit(solution)/shard_map/image_steps/pallas_call | solution.py:465
  60.9 1.8 %copy.14 = f32[16,6144]{1,0:T(8,128)} copy(f32[16,6144]{1,0:T(8,128)} %bitcast.21) | data formatting | bytes 786432

commit v3 on v2

--- a/solution.py
+++ b/solution.py
@@ -22,17 +22,15 @@
 
 
 def constants():
-    first = np.zeros((384, 768), np.float32)
+    first = np.zeros((2, 384, 384), np.float32)
     for core in range(2):
-        for y in range(4):
-            for zh in range(4):
-                block = (y * 4 + zh) * 2 + core
-                slot = (core * 4 + y) * 4 + zh
-                for r in range(8):
-                    first[block * 12 + r, slot * 8 + r] = 1.0
-                for r in range(4):
-                    first[block * 12 + 8 + r, 256 + slot * 8 + r] = 1.0
-                    first[block * 12 + 8 + r, 512 + slot * 8 + 4 + r] = 1.0
+        for slot in range(16):
+            block = slot * 2 + core
+            for r in range(8):
+                first[core, block * 12 + r, slot * 8 + r] = 1.0
+            for r in range(4):
+                first[core, block * 12 + 8 + r, 128 + slot * 8 + r] = 1.0
+                first[core, block * 12 + 8 + r, 256 + slot * 8 + 4 + r] = 1.0
     second = np.zeros((384, 384), np.float32)
     for block in range(16):
         for m in range(4):
@@ -85,7 +83,7 @@
     pres, prev, vel, core, f1, f2, dep, pf1, pf2, down, across, near_z,
     out,
     pres_v, prev_v, vel_v, core_v, f1_v, f2_v, dep_v, pf1_v, pf2_v, down_v, across_v, near_z_v,
-    kb, gb, fld, swapped, deep_z, speed, last, image, hxs, hxr, hys, hyr, v_s, w_s, g_s, t_s, bd_s, f1a_s, f1b_s, f2p_s,
+    kb, gb, fld, swapped, deep_z, speed, last, image, hxs, hxr, hys, hyr, v_s, w_s, g_s, t_s, bd_s, f1a_s, f1b_s, f2p_s, f1_r, mine, theirs, got_s,
     lsem, zs, zr, ys, yr, cs, cr, gzs, gzr, gxs, gxr, hxss, hxrs, hyss, hyrs,
 ):
     gx, gy = lax.axis_index("gx"), lax.axis_index("gy")
@@ -102,7 +100,7 @@
     ypeer = [at(y + d, zh, c) for d in (1, 2, 3)]
     cpeer = at(y, zh, 1 - c)
     lpeer = [other(x, zl + d) for d in (1, 2, 3)]
-    xpeer = [other(x + 1, zl), other(x + 3, zl)]
+    xpeer = [other(x + d, zl) for d in (1, 2, 3)]
     hx = [((gx + 31) % 32, gy), ((gx + 1) % 32, gy)]
     hy = [(gx, (gy + 15) % 16), (gx, (gy + 1) % 16)]
 
@@ -146,28 +144,24 @@
     for s in range(STEPS):
         raw = core_v[s].astype(F32)
         tail = jnp.concatenate([raw[8:12, :384], raw[8:12, 384:]], axis=0)
-        kb[s, c, y, zh] = jnp.concatenate([raw[:8], tail], axis=1).astype(BF16)
-
-    def along_z(s):
-        own = kb.at[s, c, y, zh]
-        for k in range(3):
-            to = k + jnp.where(k >= zh, 1, 0)
-            send(own, own, zs.at[s, k], zr.at[s, zh], at(y, to, c))
-
-    def along_y(s):
+        kb[s, y, zh] = jnp.concatenate([raw[:8], tail], axis=1).astype(BF16)
+    def along_z(s, k):
+        own = kb.at[s, y, zh]
+        to = k + jnp.where(k >= zh, 1, 0)
+        send(own, own, zs.at[s, k], zr.at[s, zh], at(y, to, c))
+
+    def start_y(s):
         for d in range(3):
             source = (zh + 3 - d) % 4
-            arrive(kb.at[s, c, y, source], zs.at[s, d], zr.at[s, source], zpeer[d])
-        row = kb.at[s, c, y]
+            arrive(kb.at[s, y, source], zs.at[s, d], zr.at[s, source], zpeer[d])
+        row = kb.at[s, y]
         for d in (0, 2, 1):
             send(row, row, ys.at[s, d], yr.at[s, d], ypeer[d])
-        send(row, row, cs.at[s, 3], cr.at[s, 3], cpeer)
-
-    def to_core(s):
-        for d in (0, 2, 1):
-            row = kb.at[s, c, (y + 3 - d) % 4]
-            arrive(row, ys.at[s, d], yr.at[s, d], ypeer[d])
-            send(row, row, cs.at[s, d], cr.at[s, d], cpeer)
+
+    def end_y(s):
+        for d in range(3):
+            arrive(kb.at[s, (y + 3 - d) % 4], ys.at[s, d], yr.at[s, d], ypeer[d])
+
 
     low_half = lax.broadcasted_iota(jnp.int32, (8, 128), 1) < 64
     sub = lax.broadcasted_iota(jnp.int32, (8, 128), 0)
@@ -275,14 +269,18 @@
 
     lane8 = lax.broadcasted_iota(jnp.int32, (8, 128), 1)
 
-    def partial(s):
-        arrive(kb.at[s, 1 - c, y], cs.at[s, 3], cr.at[s, 3], cpeer)
-        for d in range(3):
-            arrive(kb.at[s, 1 - c, (y + 3 - d) % 4], cs.at[s, d], cr.at[s, d], cpeer)
-        blocks = kb[s].reshape(256, 1152)
+    def multiply(s):
+        blocks = kb[s].reshape(128, 1152)
         top = dot(f1a_s[...], blocks[:, :768])
         low = dot(f1b_s[...], blocks[:, 768:])
-        value = top + jnp.concatenate([low[:16], low[16:]], axis=1)
+        value = top + jnp.concatenate([low[:32], low[32:]], axis=1)
+        mine[s] = value[:16]
+        theirs[s] = value[16:]
+        send(theirs.at[s], got_s.at[s], cs.at[s], cr.at[s], cpeer)
+
+    def partial(s):
+        arrive(got_s.at[s], cs.at[s], cr.at[s], cpeer)
+        value = mine[s] + got_s[s]
         largest = jnp.max(jnp.abs(value), axis=(0, 1), keepdims=True)
         largest = jnp.maximum(largest * 1.01, 1e-30).astype(BF16).astype(F32)
         code = encode(value, LIFT / largest)
@@ -305,6 +303,8 @@
         own = gb.at[s, x, zl]
         for d in range(3):
             send(own, own, gzs.at[s, d], gzr.at[s, d], lpeer[d])
+        for d in (0, 2, 1):
+            send(own, own, gxs.at[s, d, 3], gxr.at[s, d, zl], xpeer[d])
 
     def decode_row(s, row):
         def block(b, carry):
@@ -319,27 +319,20 @@
         lax.fori_loop(0, 4, block, 0)
 
     def start_x(s):
-        for d in range(3):
-            arrive(gb.at[s, x, (zl + 3 - d) % 4], gzs.at[s, d], gzr.at[s, d], lpeer[d])
-        row = gb.at[s, x]
-        for side in range(2):
-            send(row, row, gxs.at[s, side], gxr.at[s, side], xpeer[side])
+        for d in (0, 2, 1):
+            block = gb.at[s, x, (zl + 3 - d) % 4]
+            arrive(block, gzs.at[s, d], gzr.at[s, d], lpeer[d])
+            for e in (0, 2, 1):
+                send(block, block, gxs.at[s, e, d], gxr.at[s, e, (zl + 3 - d) % 4], xpeer[e])
         decode_row(s, x)
 
-    def forward_x(s):
-        for side in range(2):
-            source = (x + 3 - 2 * side) % 4
-            arrive(gb.at[s, source], gxs.at[s, side], gxr.at[s, side], xpeer[side])
-            half = gb.at[s, source, pl.ds(2 * side, 2)]
-            send(half, half, gxs.at[s, 2 + side], gxr.at[s, 2 + side], xpeer[side])
-        for side in range(2):
-            decode_row(s, (x + 3 - 2 * side) % 4)
+    def end_x(s, d):
+        source = (x + 3 - d) % 4
+        for i in range(4):
+            arrive(gb.at[s, source, i], gxs.at[s, d, i], gxr.at[s, d, i], xpeer[d])
+        decode_row(s, source)
 
     def finish(s):
-        for side in range(2):
-            half = gb.at[s, (x + 2) % 4, pl.ds(2 * side, 2)]
-            arrive(half, gxs.at[s, 2 + side], gxr.at[s, 2 + side], xpeer[side])
-        decode_row(s, (x + 2) % 4)
         high, low = halves(g_s[s])
         mixed = dot(f2p_s[...], high) + dot(f2p_s[...], low)
         high, low = halves(mixed)
@@ -378,10 +371,7 @@
     def prepare():
         for load in loads[4:11]:
             load.wait()
-        f1p = dot(f1_v[...], pf1_v[...]).astype(BF16)
-        f1a_s[...] = f1p[:, :256]
-        f1b_s[0:16] = f1p[:, 256:512]
-        f1b_s[16:32] = f1p[:, 512:768]
+        send(f1_v, f1_r, cs.at[STEPS], cr.at[STEPS], cpeer)
         f2p_s[...] = dot(f2_v[...], pf2_v[...]).astype(BF16)
         tall = dot(down_v[...], dep_v[...])
         wide = dot(tall.astype(BF16), across_v[...])
@@ -393,6 +383,14 @@
             bd_s[0:128, 256 * i : 256 * i + 256] = part
             bd_s[128:256, 256 * i : 256 * i + 256] = part
 
+    def prepare_first():
+        arrive(f1_r, cs.at[STEPS], cr.at[STEPS], cpeer)
+        both = jnp.concatenate([f1_v[...], f1_r[...]], axis=0)
+        both = dot(both, pf1_v[c]).astype(BF16)
+        f1a_s[...] = both[:, :128]
+        f1b_s[0:32] = both[:, 128:256]
+        f1b_s[32:64] = both[:, 256:384]
+
     def first_fields():
         loads[1].wait()
 
@@ -418,38 +416,53 @@
         loads[2].wait()
 
     pl.semaphore_wait(barrier, len(everyone))
-    along_z(0)
+    along_z(0, 0)
+    along_z(0, 1)
+    along_z(0, 2)
     first_fields()
+    prepare()
+    flush(3)
+    along_z(1, 0)
+    along_z(1, 1)
+    along_z(1, 2)
     send_halo(0)
-    flush(3)
-    along_z(1)
-    prepare()
     loads[11].wait()
     inner(0)
-    flush(4)
     flush(3)
-    along_z(2)
+    along_z(2, 0)
+    along_z(2, 1)
+    along_z(2, 2)
     speeds()
-    along_y(0)
-    along_y(1)
-    to_core(0)
+    prepare_first()
+    start_y(0)
+    start_y(1)
+    end_y(0)
+    multiply(0)
     step(0)
-    along_y(2)
+    start_y(2)
     partial(0)
-    to_core(1)
+    end_y(1)
+    multiply(1)
     partial(1)
+    end_y(2)
+    multiply(2)
     start_x(0)
-    to_core(2)
+    step(1)
     partial(2)
     start_x(1)
-    forward_x(0)
-    step(1)
+    end_x(0, 0)
+    end_x(0, 2)
     start_x(2)
-    forward_x(1)
+    end_x(1, 0)
+    end_x(1, 2)
+    end_x(0, 1)
     finish(0)
-    forward_x(2)
     step(2)
+    end_x(2, 0)
+    end_x(2, 2)
+    end_x(1, 1)
     finish(1)
+    end_x(2, 1)
     finish(2)
     flush()
 
@@ -464,14 +477,14 @@
     dma = pltpu.SemaphoreType.DMA
     image = pl.pallas_call(
         kernel,
-        out_shape=jax.ShapeDtypeStruct((CX * TILES, 128), F32),
+        out_shape=pltpu.VMEM((CX * TILES, 128), F32),
         in_specs=[pl.BlockSpec(memory_space=pl.ANY)] * len(args),
         out_specs=pl.BlockSpec(memory_space=pltpu.VMEM),
         scratch_shapes=[
             pltpu.VMEM(a.shape, a.dtype) for a in args
         ]
         + [
-            pltpu.VMEM((STEPS, 2, 4, 4, 8, 1152), BF16),
+            pltpu.VMEM((STEPS, 4, 4, 8, 1152), BF16),
             pltpu.VMEM((STEPS, 4, 4, 16, 896), BF16),
             pltpu.VMEM((STEPS, 24 * 10 * 8, 128), F32),
             pltpu.VMEM((24 * 10 * 8, 128), F32),
@@ -488,15 +501,19 @@
             pltpu.VMEM((STEPS, 384, 512), F32),
             pltpu.VMEM((2 * 8 * YL, 128), F32),
             pltpu.VMEM((256, 512), BF16),
-            pltpu.VMEM((16, 256), BF16),
-            pltpu.VMEM((32, 256), BF16),
+            pltpu.VMEM((32, 128), BF16),
+            pltpu.VMEM((64, 128), BF16),
             pltpu.VMEM((YL, 384), BF16),
+            pltpu.VMEM((CX, 384), BF16),
+            pltpu.VMEM((STEPS, CX, 768), F32),
+            pltpu.VMEM((STEPS, CX, 768), F32),
+            pltpu.VMEM((STEPS, CX, 768), F32),
             dma((len(args),)),
             dma((STEPS, 3)), dma((STEPS, 4)),
+            dma((STEPS, 4)), dma((STEPS, 4)),
+            dma((STEPS + 1,)), dma((STEPS + 1,)),
             dma((STEPS, 3)), dma((STEPS, 3)),
-            dma((STEPS, 4)), dma((STEPS, 4)),
-            dma((STEPS, 3)), dma((STEPS, 3)),
-            dma((STEPS, 4)), dma((STEPS, 4)),
+            dma((STEPS, 3, 4)), dma((STEPS, 3, 4)),
             dma((STEPS, 2)), dma((STEPS, 2)),
             dma((STEPS, 2)), dma((STEPS, 2)),
         ],

time: 62.9 us -> 57.7 us (0.917); the launches traced: 62.7 us -> 56.8 us
  Pallas kernels: 60.9 us -> 56 us
  local copies, waits for them, and re-layouts: 1.77 us -> 0.75 us
    pallas_call x1, Pallas kernels: 60.9 us -> 56 us  [body(): pl.pallas_call(kernel, out_shape=pltpu.VMEM((CX * TILES, 128), F32), in_s...]
    unnamed x1, local copies, waits for them, and re-layouts: 1.77 us -> 0.75 us
where the time goes in v3:
time: 57.7 us; the launch traced here: 56.8 us
  Pallas kernels  56 us (97%)
  local copies, waits for them, and re-layouts  0.75 us (1%)
    pallas_call x1, Pallas kernels, body(): pl.pallas_call(kernel, out_shape=pltpu.VMEM((CX * TILES, 128), F32), in_s...  56 us

profile of v3, /device:TPU:1, one launch (start us, length us, event | category | flops | bytes accessed | tf_op | source)
XLA Modules:
  0.0 56.8 jit_solution(2706399524270251016)
XLA Ops:
  0.0 56.0 %image_steps.1 = f32[768,128]{1,0:T(8,128)S(1)} custom-call(f32[768,128]{1,0:T(8,128)} %bitcast.22, f32[768,128]{1,0:T(8,128)} %bitcast.23, bf16[768,128]{1,0:T(8,128)(2,1)} %bitcast.24, bf16[3,12,768]{2,1,0:T(8,128)(2,1)} %core.1, bf16[16,384]{1,0:T(8,128)(2,1)} %f1.1, bf16[96,384]{1,0:T(8,128)(2,1)} %f2.1, bf16[32,64]{1,0:T(8,128)(2,1)} %bitcast.25, ...), custom_call_target="tpu_custom_call" | custom-call | tf_op jit(solution)/shard_map/image_steps/pallas_call | solution.py:478
  56.1 0.7 %copy.14 = f32[16,6144]{1,0:T(8,128)} copy(f32[16,6144]{1,0:T(8,128)S(1)} %bitcast.21) | data formatting | bytes 786432

commit v4 on v3

--- a/solution.py
+++ b/solution.py
@@ -83,7 +83,7 @@
     pres, prev, vel, core, f1, f2, dep, pf1, pf2, down, across, near_z,
     out,
     pres_v, prev_v, vel_v, core_v, f1_v, f2_v, dep_v, pf1_v, pf2_v, down_v, across_v, near_z_v,
-    kb, gb, fld, swapped, deep_z, speed, last, image, hxs, hxr, hys, hyr, v_s, w_s, g_s, t_s, bd_s, f1a_s, f1b_s, f2p_s, f1_r, mine, theirs, got_s,
+    kb, gb, fld, swapped, deep_z, speed, last, image, hxs, hxr, hys, hyr, v_s, w_s, g_s, mixed_s, t_s, bd_s, f1a_s, f1b_s, f2p_s, f1_r, mine, theirs, got_s,
     lsem, zs, zr, ys, yr, cs, cr, gzs, gzr, gxs, gxr, hxss, hxrs, hyss, hyrs,
 ):
     gx, gy = lax.axis_index("gx"), lax.axis_index("gy")
@@ -103,11 +103,6 @@
     xpeer = [other(x + d, zl) for d in (1, 2, 3)]
     hx = [((gx + 31) % 32, gy), ((gx + 1) % 32, gy)]
     hy = [(gx, (gy + 15) % 16), (gx, (gy + 1) % 16)]
-
-    barrier = pltpu.get_barrier_semaphore()
-    everyone = zpeer + ypeer + [cpeer] + lpeer + xpeer + hx + hy
-    for peer in everyone:
-        pl.semaphore_signal(barrier, inc=1, device_id=peer, device_id_type=MESH)
 
     loads = [
         pltpu.make_async_copy(a, b, lsem.at[i])
@@ -118,7 +113,12 @@
             ]
         )
     ]
-    for load in loads:
+    loads[0].start()
+    barrier = pltpu.get_barrier_semaphore()
+    everyone = zpeer + ypeer + [cpeer] + lpeer + xpeer + hx + hy
+    for peer in everyone:
+        pl.semaphore_signal(barrier, inc=1, device_id=peer, device_id_type=MESH)
+    for load in loads[1:]:
         load.start()
 
     def remote(src, dst, ssem, rsem, peer):
@@ -297,26 +297,27 @@
                     piece = pltpu.roll(piece, shift, 1) if shift else piece
                     chunk = piece if t == 0 else jnp.where(lane8 < 32 * t, chunk, piece)
                 w_s[6 * m : 6 * m + 6, 128 * j : 128 * j + 128] = chunk[0:6]
-        fold = jnp.concatenate([w_s[16:24, 0:256], w_s[16:24, 256:512]], axis=0)
-        mark = jnp.broadcast_to(largest, (16, 128))
-        gb[s, x, zl] = jnp.concatenate([w_s[0:16, :], fold, mark], axis=1).astype(BF16)
+        mark = jnp.broadcast_to(largest, (8, 128))
+        gb[s, x, zl] = jnp.concatenate([w_s[0:8, :], w_s[8:16, :], w_s[16:24, :], mark], axis=1).astype(BF16)
         own = gb.at[s, x, zl]
         for d in range(3):
             send(own, own, gzs.at[s, d], gzr.at[s, d], lpeer[d])
         for d in (0, 2, 1):
             send(own, own, gxs.at[s, d, 3], gxr.at[s, d, zl], xpeer[d])
 
-    def decode_row(s, row):
+    def decode_row(s, row, fresh=False):
         def block(b, carry):
             got = gb[s, row, b].astype(F32)
-            scale = got[:, 768:896] * (1.0 / LIFT)
-            value = jnp.concatenate([decode(got[:, 128 * q : 128 * q + 128], scale) for q in range(6)], axis=1)
-            start = (row * 4 + b) * 24
-            g_s[s, rows(start, 16), :] = value[:, :512]
-            g_s[s, rows(start + 16), :] = jnp.concatenate([value[0:8, 512:768], value[8:16, 512:768]], axis=1)
+            scale = got[:, 1536:1664] * (1.0 / LIFT)
+            for q in range(12):
+                value = decode(got[:, 128 * q : 128 * q + 128], scale)
+                g_s[rows(b * 24 + q // 4 * 8), 128 * (q % 4) : 128 * (q % 4) + 128] = value
             return carry
 
         lax.fori_loop(0, 4, block, 0)
+        high, low = halves(g_s[...])
+        part = dot(f2p_s[row], jnp.concatenate([high, low], axis=0))
+        mixed_s[s] = part if fresh else mixed_s[s] + part
 
     def start_x(s):
         for d in (0, 2, 1):
@@ -324,7 +325,7 @@
             arrive(block, gzs.at[s, d], gzr.at[s, d], lpeer[d])
             for e in (0, 2, 1):
                 send(block, block, gxs.at[s, e, d], gxr.at[s, e, (zl + 3 - d) % 4], xpeer[e])
-        decode_row(s, x)
+        decode_row(s, x, True)
 
     def end_x(s, d):
         source = (x + 3 - d) % 4
@@ -333,9 +334,7 @@
         decode_row(s, source)
 
     def finish(s):
-        high, low = halves(g_s[s])
-        mixed = dot(f2p_s[...], high) + dot(f2p_s[...], low)
-        high, low = halves(mixed)
+        high, low = halves(mixed_s[s])
         for j in range(4):
             cols = slice(128 * j, 128 * j + 128)
             deep = dot(jnp.concatenate([high[:, cols], low[:, cols]], axis=1), bd_s[...])
@@ -372,7 +371,10 @@
         for load in loads[4:11]:
             load.wait()
         send(f1_v, f1_r, cs.at[STEPS], cr.at[STEPS], cpeer)
-        f2p_s[...] = dot(f2_v[...], pf2_v[...]).astype(BF16)
+        f2p = dot(f2_v[...], pf2_v[...]).astype(BF16)
+        for row in range(4):
+            part = f2p[:, 96 * row : 96 * row + 96]
+            f2p_s[row] = jnp.concatenate([part, part], axis=1)
         tall = dot(down_v[...], dep_v[...])
         wide = dot(tall.astype(BF16), across_v[...])
         block_row = lax.broadcasted_iota(jnp.int32, (128, 256), 0) // 32
@@ -438,30 +440,30 @@
     start_y(1)
     end_y(0)
     multiply(0)
+    partial(0)
+    start_y(2)
     step(0)
-    start_y(2)
-    partial(0)
     end_y(1)
     multiply(1)
     partial(1)
+    start_x(0)
     end_y(2)
     multiply(2)
-    start_x(0)
-    step(1)
     partial(2)
     start_x(1)
+    step(1)
+    start_x(2)
     end_x(0, 0)
     end_x(0, 2)
-    start_x(2)
+    end_x(0, 1)
+    finish(0)
     end_x(1, 0)
     end_x(1, 2)
-    end_x(0, 1)
-    finish(0)
     step(2)
+    end_x(1, 1)
+    finish(1)
     end_x(2, 0)
     end_x(2, 2)
-    end_x(1, 1)
-    finish(1)
     end_x(2, 1)
     finish(2)
     flush()
@@ -485,7 +487,7 @@
         ]
         + [
             pltpu.VMEM((STEPS, 4, 4, 8, 1152), BF16),
-            pltpu.VMEM((STEPS, 4, 4, 16, 896), BF16),
+            pltpu.VMEM((STEPS, 4, 4, 8, 1664), BF16),
             pltpu.VMEM((STEPS, 24 * 10 * 8, 128), F32),
             pltpu.VMEM((24 * 10 * 8, 128), F32),
             pltpu.VMEM((CX * TILES, 128), F32),
@@ -498,12 +500,13 @@
             pltpu.VMEM((STEPS, 2, 2, CX, 128), F32),
             pltpu.VMEM((128, 128), F32),
             pltpu.VMEM((24, 512), F32),
-            pltpu.VMEM((STEPS, 384, 512), F32),
+            pltpu.VMEM((96, 512), F32),
+            pltpu.VMEM((STEPS, YL, 512), F32),
             pltpu.VMEM((2 * 8 * YL, 128), F32),
             pltpu.VMEM((256, 512), BF16),
             pltpu.VMEM((32, 128), BF16),
             pltpu.VMEM((64, 128), BF16),
-            pltpu.VMEM((YL, 384), BF16),
+            pltpu.VMEM((4, YL, 192), BF16),
             pltpu.VMEM((CX, 384), BF16),
             pltpu.VMEM((STEPS, CX, 768), F32),
             pltpu.VMEM((STEPS, CX, 768), F32),

time: 57.7 us -> 55.5 us (0.962)
  Pallas kernels: 56 us -> 54.4 us
    pallas_call x1, Pallas kernels: 56 us -> 54.4 us  [body(): pl.pallas_call(kernel, out_shape=pltpu.VMEM((CX * TILES, 128), F32), in_s...]
where the time goes in v4:
time: 55.5 us; the launch traced here: 55.1 us
  Pallas kernels  54.4 us (98%)
  local copies, waits for them, and re-layouts  0.75 us (1%)
    pallas_call x1, Pallas kernels, body(): pl.pallas_call(kernel, out_shape=pltpu.VMEM((CX * TILES, 128), F32), in_s...  54.4 us

profile of v4, /device:TPU:1, one launch (start us, length us, event | category | flops | bytes accessed | tf_op | source)
XLA Modules:
  0.0 55.1 jit_solution(13431463083990716954)
XLA Ops:
  0.0 54.4 %image_steps.1 = f32[768,128]{1,0:T(8,128)S(1)} custom-call(f32[768,128]{1,0:T(8,128)} %bitcast.22, f32[768,128]{1,0:T(8,128)} %bitcast.23, bf16[768,128]{1,0:T(8,128)(2,1)} %bitcast.24, bf16[3,12,768]{2,1,0:T(8,128)(2,1)} %core.1, bf16[16,384]{1,0:T(8,128)(2,1)} %f1.1, bf16[96,384]{1,0:T(8,128)(2,1)} %f2.1, bf16[32,64]{1,0:T(8,128)(2,1)} %bitcast.25, ...), custom_call_target="tpu_custom_call" | custom-call | tf_op jit(solution)/shard_map/image_steps/pallas_call | solution.py:480
  54.4 0.7 %copy.14 = f32[16,6144]{1,0:T(8,128)} copy(f32[16,6144]{1,0:T(8,128)S(1)} %bitcast.21) | data formatting | bytes 786432

commit v5 on v4

--- a/solution.py
+++ b/solution.py
@@ -155,7 +155,7 @@
             source = (zh + 3 - d) % 4
             arrive(kb.at[s, y, source], zs.at[s, d], zr.at[s, source], zpeer[d])
         row = kb.at[s, y]
-        for d in (0, 2, 1):
+        for d in (1, 0, 2):
             send(row, row, ys.at[s, d], yr.at[s, d], ypeer[d])
 
     def end_y(s):
@@ -302,7 +302,7 @@
         own = gb.at[s, x, zl]
         for d in range(3):
             send(own, own, gzs.at[s, d], gzr.at[s, d], lpeer[d])
-        for d in (0, 2, 1):
+        for d in (1, 0, 2):
             send(own, own, gxs.at[s, d, 3], gxr.at[s, d, zl], xpeer[d])
 
     def decode_row(s, row, fresh=False):
@@ -323,7 +323,7 @@
         for d in (0, 2, 1):
             block = gb.at[s, x, (zl + 3 - d) % 4]
             arrive(block, gzs.at[s, d], gzr.at[s, d], lpeer[d])
-            for e in (0, 2, 1):
+            for e in (1, 0, 2):
                 send(block, block, gxs.at[s, e, d], gxr.at[s, e, (zl + 3 - d) % 4], xpeer[e])
         decode_row(s, x, True)
 

time: 55.5 us -> 54.9 us (0.989)
  Pallas kernels: 54.4 us -> 53.6 us
    pallas_call x1, Pallas kernels: 54.4 us -> 53.6 us  [body(): pl.pallas_call(kernel, out_shape=pltpu.VMEM((CX * TILES, 128), F32), in_s...]
where the time goes in v5:
time: 54.9 us; the launch traced here: 54.4 us
  Pallas kernels  53.6 us (98%)
  local copies, waits for them, and re-layouts  0.75 us (1%)
    pallas_call x1, Pallas kernels, body(): pl.pallas_call(kernel, out_shape=pltpu.VMEM((CX * TILES, 128), F32), in_s...  53.6 us

profile of v5, /device:TPU:1, one launch (start us, length us, event | category | flops | bytes accessed | tf_op | source)
XLA Modules:
  0.0 54.4 jit_solution(17302469815571970047)
XLA Ops:
  0.0 53.6 %image_steps.1 = f32[768,128]{1,0:T(8,128)S(1)} custom-call(f32[768,128]{1,0:T(8,128)} %bitcast.22, f32[768,128]{1,0:T(8,128)} %bitcast.23, bf16[768,128]{1,0:T(8,128)(2,1)} %bitcast.24, bf16[3,12,768]{2,1,0:T(8,128)(2,1)} %core.1, bf16[16,384]{1,0:T(8,128)(2,1)} %f1.1, bf16[96,384]{1,0:T(8,128)(2,1)} %f2.1, bf16[32,64]{1,0:T(8,128)(2,1)} %bitcast.25, ...), custom_call_target="tpu_custom_call" | custom-call | tf_op jit(solution)/shard_map/image_steps/pallas_call | solution.py:480
  53.6 0.7 %copy.14 = f32[16,6144]{1,0:T(8,128)} copy(f32[16,6144]{1,0:T(8,128)S(1)} %bitcast.21) | data formatting | bytes 786432
